TPU v7x, 32 devices: a whole 2x2x4 slice. The times are simulated.
32 devices in a mesh: pool: 8 (over z, core), tensor: 4 (over y, x).
Axes of the slice: x: 2, y: 2, z: 4, core: 2. Of those that a mesh axis runs over, the one named last changes fastest.
Arguments:
- hidden: bfloat16 [4096, 14336], P('pool', 'tensor'), may hold values from -6 to 6
- down_weight: bfloat16 [14336, 8192], P('tensor', 'pool'), may hold values from -0.046875 to 0.046875
- adapter_shrink: bfloat16 [16, 14336, 64], P('pool', 'tensor'), may hold values from -0.046875 to 0.046875
- adapter_expand: bfloat16 [16, 8192, 64], P('pool', 'tensor'), may hold values from -0.75 to 0.75
- block_adapter: int32 [32], P('pool'), may hold values from 0 to 15, as said below
- block_rows: int32 [32], P('pool'), may hold values from 1 to 128, 3072 in all
Outputs:
- projected: bfloat16 [4096, 8192], P(('pool', 'tensor'))
Inputs may be any that keep to these rules, and one draw needn't show every extreme that they name: `block_adapter`: within each aligned run of 4 blocks (the rows of one pool index) no two blocks name adapters with the same a // 2. `block_rows`: some block is full.
All inputs are finite; a program needn't handle non-finite values.
Results may differ from a plain program's by a relative error of at most 0.02.
Values may be sent and summed in bfloat16 or wider, within the bound.
No kernel may reach another device: no remote copies, remote signals or barrier semaphores. Data moves between devices by JAX's collectives and lax.ppermute only.
A program may use at most 128 MiB of HBM per device.

v0:
```python
import functools

import jax
import jax.numpy as jnp
from jax import lax
from jax.experimental import pallas as pl
from jax.experimental.pallas import tpu as pltpu
from jax.sharding import PartitionSpec as P

BLOCK = 128
SCALE = 0.5


def general(hidden, down_weight, adapter_shrink, adapter_expand, block_adapter, block_rows):
    input_rows, feat = hidden.shape
    block_count = block_adapter.shape[0]
    column_span = adapter_expand.shape[1]
    tensor_pos = lax.axis_index("tensor")
    tensor_count = lax.axis_size("tensor")
    own_rows = input_rows // tensor_count
    blocks = hidden.reshape(block_count, BLOCK, feat)
    partial_value = jnp.dot(
        hidden,
        lax.all_gather(down_weight, "pool", axis=1, tiled=True),
        preferred_element_type=jnp.float32,
    )
    total = lax.psum_scatter(
        partial_value.astype(jnp.bfloat16), "tensor", scatter_dimension=0, tiled=True
    ).astype(jnp.float32)
    shrink_piece = lax.all_gather(adapter_shrink, "pool", axis=0, tiled=True)
    expand_piece = lax.all_gather(adapter_expand, "pool", axis=0, tiled=True)
    idents = jnp.arange(shrink_piece.shape[0], dtype=jnp.int32)
    pick = (block_adapter[:, None] == idents[None, :]).astype(jnp.bfloat16)
    first = jnp.einsum("bk,kfr->bfr", pick, shrink_piece, preferred_element_type=jnp.float32)
    second = jnp.einsum("bk,kcr->bcr", pick, expand_piece, preferred_element_type=jnp.float32)
    shrink = jnp.einsum(
        "bnf,bfr->bnr", blocks, first.astype(jnp.bfloat16), preferred_element_type=jnp.float32
    )
    summed_shrink = lax.psum(shrink.astype(jnp.bfloat16), "tensor")
    enlarged_rows = jnp.einsum(
        "bnr,bcr->bnc",
        summed_shrink,
        second.astype(jnp.bfloat16),
        preferred_element_type=jnp.float32,
    )
    adapter_delta_columns = (
        (SCALE * enlarged_rows).astype(jnp.bfloat16).reshape(input_rows, column_span)
    )
    delta_mine = lax.all_to_all(
        adapter_delta_columns, "tensor", split_axis=0, concat_axis=1, tiled=True
    )
    total = total + delta_mine.astype(jnp.float32)
    row_ids = tensor_pos * own_rows + jnp.arange(own_rows, dtype=jnp.int32)
    owning = (row_ids // BLOCK)[:, None] == jnp.arange(block_count, dtype=jnp.int32)[None, :]
    lengths = jnp.sum(jnp.where(owning, block_rows[None, :], 0), axis=1)
    valid = (row_ids % BLOCK < lengths).astype(jnp.float32)
    return (total * valid[:, None]).astype(jnp.bfloat16)


def dot(a, b):
    return jnp.dot(a, b, preferred_element_type=jnp.float32)


def on_line(pairs):
    return [(2 * a + c, 2 * b + c) for a, b in pairs for c in range(2)]


XOR = {s: on_line([(z, z ^ s) for z in range(4)]) for s in (1, 2, 3)}
MIDDLE = on_line([(1, 2), (2, 1)])
OUTWARD = on_line([(1, 0), (2, 3)])
INWARD = on_line([(0, 1), (3, 2)])
ACROSS = on_line([(1, 3), (2, 0)])
SIBLING = [(p, p ^ 1) for p in range(8)]

TILE = 512
NEAR = 4 * TILE
WIDE = 2048
SHARE = 512
INNER, CORE, ZPOS, NAMES = 0, 1, 2, 3
CHEAP = pl.CostEstimate(flops=1000, bytes_accessed=1000, transcendentals=0)


def send(x, pairs):
    return lax.ppermute(x, "pool", pairs)


def after(events, *xs):
    tied = lax.optimization_barrier((tuple(events), xs))
    return tied[1] if len(xs) > 1 else tied[1][0]


def params(limit):
    return pltpu.CompilerParams(vmem_limit_bytes=limit * 1024 * 1024)


class Rows:
    def __init__(self, parts, role, at):
        self.parts, self.role, self.at = parts, role, at
        self.rows = parts[0][0].shape[0]
        self.total = sum(part[2] for part in parts)


def block_sums(meta, slot, low, start, count, b):
    name = meta[NAMES + 4 * slot + b]
    chip = name >> 2
    place = ((((name >> 1) & 1) ^ meta[CORE]) << 2) + jnp.where(chip == meta[ZPOS], 0, 2) + (name & 1)
    place = jnp.where((chip == meta[ZPOS]) | (chip == (meta[ZPOS] ^ 1)), place, -1)
    value = jnp.zeros((count, 64), jnp.float32)
    for i in range(8):
        part = low[start + b * count : start + (b + 1) * count, i * 64 : i * 64 + 64]
        value = value + jnp.where(place == i, part, 0.0)
    return value.astype(jnp.bfloat16)


def accumulate(ref, rows, cols, value, k, first):
    if first:
        value = value + jnp.where(k == 0, 0.0, ref[rows, cols])
    else:
        value = value + ref[rows, cols]
    ref[rows, cols] = value


def times_transposed(x, a):
    return lax.dot_general(x, a, (((1,), (1,)), ((), ())), preferred_element_type=jnp.float32)


def products_kernel(jobs, weights, meta, *refs):
    refs = list(refs)
    xs = [[refs.pop(0) for _ in job.parts] for job in jobs]
    ws = [(refs.pop(0), refs.pop(0)) for _ in range(weights)]
    out, acc = refs
    k = pl.program_id(0)
    top = {0: 0, 1: 0}
    for x_parts, job in zip(xs, jobs):
        start = max(top.values()) if job.role is None else top[job.role]
        for role in top if job.role is None else (job.role,):
            top[role] = start + job.rows
        mine = slice(start, start + job.rows)
        role = True if job.role is None else meta[INNER] == job.role
        base = 0
        for x, (_, _, tiles, weight) in zip(x_parts, job.parts):

            def step(x=x, mine=mine, pair=ws[weight], first=base == 0):
                for h, w in enumerate(pair):
                    for n in range(0, WIDE // 2, 512):
                        at = slice(h * (WIDE // 2) + n, h * (WIDE // 2) + n + 512)
                        accumulate(acc, mine, at, dot(x[...], w[:, n : n + 512]), k, first)

            pl.when(role & (k >= base) & (k < base + tiles))(step)
            base += tiles

        def store(job=job, start=start):
            count = job.rows // 4
            for b in range(4):
                value = acc[start + b * count : start + (b + 1) * count, :]
                out[b, job.at : job.at + count, :] = value.astype(jnp.bfloat16)

        pl.when(role & (k == job.total - 1))(store)


def products(meta, jobs, weights, rows):
    steps = max(job.total for job in jobs)
    in_specs, args, uses = [], [], {}
    for job in jobs:
        base = 0
        for x, tile, tiles, weight in job.parts:

            def index(k, m, base=base, tile=tile, tiles=tiles, role=job.role):
                at = jnp.clip(k - base, 0, tiles - 1)
                if role is not None:
                    at = at * (m[INNER] if role == 1 else 1 - m[INNER])
                return (0, at + tile)

            in_specs.append(pl.BlockSpec((x.shape[0], TILE), index))
            args.append(x)
            for role in (0, 1) if job.role is None else (job.role,):
                uses[weight, role] = (base, tiles)
            base += tiles
    for i, (own, own_tile, other, other_tile) in enumerate(weights):
        for w, tile in ((own, own_tile), (other, other_tile)):

            def index(k, m, i=i, tile=tile):
                at = [jnp.clip(k - base, 0, tiles - 1) for base, tiles in (uses.get((i, r), (0, 1)) for r in (0, 1))]
                return (jnp.where(m[INNER] == 1, at[1], at[0]) + tile, 0)

            in_specs.append(pl.BlockSpec((TILE, w.shape[1]), index))
            args.append(w)
    both = sum(job.rows for job in jobs if job.role is None)
    height = both + max(sum(job.rows for job in jobs if job.role == r) for r in (0, 1))
    shape = (4, rows, WIDE)
    return pl.pallas_call(
        functools.partial(products_kernel, jobs, len(weights)),
        grid_spec=pltpu.PrefetchScalarGridSpec(
            num_scalar_prefetch=1,
            grid=(steps,),
            in_specs=in_specs,
            out_specs=pl.BlockSpec(shape, lambda k, m: (0, 0, 0)),
            scratch_shapes=[pltpu.VMEM((height, WIDE), jnp.float32)],
        ),
        out_shape=pltpu.HBM(shape, jnp.bfloat16),
        compiler_params=params(50),
        cost_estimate=CHEAP,
    )(meta, *args)


def shrink_kernel(tiles, slots, steps, meta, *refs):
    refs = list(refs)
    xs = [[refs.pop(0) for _ in part] for part in tiles]
    mine, other, held_mine, held_other, out, low = refs
    k = pl.program_id(0)
    inner = meta[INNER] == 1
    rows = BLOCK * 4
    for i, x_parts in enumerate(xs):
        base = 0
        for x, count in zip(x_parts, tiles[i]):

            @pl.when(inner & (k >= base) & (k < base + count))
            def _(i=i, x=x, first=base == 0):
                here = slice(i * rows, (i + 1) * rows)
                for h, a in enumerate((mine, other)):
                    accumulate(low, here, slice(h * 256, h * 256 + 256), times_transposed(x[...], a[...]), k, first)

            base += count

    @pl.when(inner & (k == steps - 1))
    def _():
        for i, slot in enumerate(slots):
            for b in range(4):
                at = 2 * SHARE + i * 64
                out[b, :, at : at + 64] = block_sums(meta, slot, low, i * rows, BLOCK, b)

    @pl.when(k == 0)
    def _():
        for b in range(4):
            for slot in range(4):
                name = meta[NAMES + 4 * slot + b]
                index = 2 * ((name >> 2) ^ meta[ZPOS]) + (name & 1)
                value = jnp.where(((name >> 1) & 1) == meta[CORE], held_mine[index], held_other[index])
                at = slot // 2 * SHARE
                out[b, slot % 2 * 64 : slot % 2 * 64 + 64, at : at + SHARE] = value


def shrink_sums(meta, xs, slots, mine, other, held):
    tiles = [[part.shape[1] // TILE for part in x] for x in xs]
    steps = sum(tiles[0])
    in_specs, args = [], []
    for x, counts in zip(xs, tiles):
        base = 0
        for part, count in zip(x, counts):

            def index(k, m, base=base, count=count):
                return (0, jnp.clip(k - base, 0, count - 1) * m[INNER])

            in_specs.append(pl.BlockSpec((part.shape[0], TILE), index))
            args.append(part)
            base += count
    for a in (mine, other):
        in_specs.append(pl.BlockSpec((a.shape[0], TILE), lambda k, m: (0, k * m[INNER])))
        args.append(a)
    for a in held:
        in_specs.append(pl.BlockSpec(a.shape, lambda k, m: (0, 0, 0)))
        args.append(a)
    shape = (4, BLOCK, 2 * SHARE + 256)
    return pl.pallas_call(
        functools.partial(shrink_kernel, tiles, slots, steps),
        grid_spec=pltpu.PrefetchScalarGridSpec(
            num_scalar_prefetch=1,
            grid=(steps,),
            in_specs=in_specs,
            out_specs=pl.BlockSpec(shape, lambda k, m: (0, 0, 0)),
            scratch_shapes=[pltpu.VMEM((4 * BLOCK * len(xs), 512), jnp.float32)],
        ),
        out_shape=pltpu.HBM(shape, jnp.bfloat16),
        compiler_params=params(40),
        cost_estimate=CHEAP,
    )(meta, *args)


def low_kernel(x, out, swapped):
    value = x[0].astype(jnp.float32)
    for b in range(1, 4):
        value = value + x[b].astype(jnp.float32)
    value = value.astype(jnp.bfloat16)
    out[...] = value
    swapped[...] = jnp.concatenate([value[:, i * 64 : i * 64 + 64] for i in (1, 0, 3, 2)], axis=1)


def low_sums(x):
    shape = jax.ShapeDtypeStruct((BLOCK, 256), jnp.bfloat16)
    whole = pl.BlockSpec((BLOCK, 256), lambda i: (0, 0))
    return pl.pallas_call(
        low_kernel,
        grid=(1,),
        in_specs=[pl.BlockSpec((4, BLOCK, 256), lambda i: (0, 0, 2 * SHARE // 256))],
        out_specs=(whole, whole),
        out_shape=(shape, shape),
        cost_estimate=CHEAP,
    )(x)


def add_kernel(x, y, out):
    out[...] = (x[...].astype(jnp.float32) + y[...].astype(jnp.float32)).astype(jnp.bfloat16)


def add(x, y):
    return pl.pallas_call(add_kernel, out_shape=jax.ShapeDtypeStruct(x.shape, x.dtype), cost_estimate=CHEAP)(x, y)


def finish_kernel(role, row, rows, lanes, has_more, meta, *refs):
    refs = list(refs)
    part = refs.pop(0)
    if lanes:
        low_in, low_out, expand = refs.pop(0), refs.pop(0), refs.pop(0)
    more = refs.pop(0) if has_more else None
    out = refs.pop(0)

    def run():
        total = part[0, row : row + rows, :].astype(jnp.float32)
        for b in range(1, 4):
            total = total + part[b, row : row + rows, :].astype(jnp.float32)
        if lanes:
            x = low_in[:rows, lanes[0] : lanes[0] + 64]
            y = low_out[:rows, lanes[1] : lanes[1] + 64]
            x = jnp.where(meta[INNER] == 1, x, y)
            delta = [dot(x, expand[i]) for i in range(expand.shape[0])]
            total = total + SCALE * jnp.concatenate(delta, axis=1)
        if has_more:
            total = total + more[...].astype(jnp.float32)
        out[...] = total.astype(jnp.bfloat16)

    if role is None:
        run()
    else:
        pl.when(meta[INNER] == role)(run)


def finish(meta, role, part, row, low=None, more=None, rows=BLOCK):
    span = WIDE // 2
    in_specs = [pl.BlockSpec((4, part.shape[1], span), lambda h, m: (0, 0, h))]
    args = [part]
    lanes = None
    if low is not None:
        *sums, expand, slots = low
        for x in sums:
            in_specs.append(pl.BlockSpec(x.shape, lambda h, m: (0, 0)))
            args.append(x)

        def index(h, m):
            slot = slots[1] + (slots[0] - slots[1]) * m[INNER]
            return (h ^ m[CORE], slot & 1, slot >> 1)

        in_specs.append(pl.BlockSpec((span // SHARE, 64, SHARE), index))
        args.append(expand)
        lanes = [64 * (0, 2, 1, 3)[slots[0]], 64 * (2, 0, 1, 3)[slots[1]]]
    if more is not None:
        in_specs.append(pl.BlockSpec((rows, span), lambda h, m: (0, h)))
        args.append(more)
    return pl.pallas_call(
        functools.partial(finish_kernel, role, row, rows, lanes, more is not None),
        grid_spec=pltpu.PrefetchScalarGridSpec(
            num_scalar_prefetch=1,
            grid=(2,),
            in_specs=in_specs,
            out_specs=pl.BlockSpec((rows, span), lambda h, m: (0, h)),
        ),
        out_shape=jax.ShapeDtypeStruct((rows, WIDE), jnp.bfloat16),
        compiler_params=params(32),
        cost_estimate=CHEAP,
    )(meta, *args)


def assemble_kernel(span, meta, count, own, one, two, inner_three, outer_three, out):
    z, c, inner = meta[ZPOS], meta[CORE], meta[INNER] == 1
    rows = own.shape[0]
    valid = lax.broadcasted_iota(jnp.int32, (rows, 1), 0) < count[0]

    def put(j, source):
        for h in range(2):
            at = pl.ds(pl.multiple_of((2 * j + h) * span, span), span)
            part = pl.ds(pl.multiple_of((h ^ c) * span, span), span)
            out[:, at] = jnp.where(valid, source[:, part], jnp.zeros((), jnp.bfloat16))

    put(z, own)
    put(z ^ 1, one)
    put(z ^ 2, two)

    @pl.when(inner)
    def _():
        put(z ^ 3, inner_three)

    @pl.when(jnp.logical_not(inner))
    def _():
        put(z ^ 3, outer_three)


def assemble(meta, count, *args):
    rows, wide = args[0].shape
    return pl.pallas_call(
        functools.partial(assemble_kernel, wide // 2),
        grid_spec=pltpu.PrefetchScalarGridSpec(
            num_scalar_prefetch=2,
            grid=(1,),
            in_specs=[pl.BlockSpec(a.shape, lambda n, m, k: (0, 0)) for a in args],
            out_specs=pl.BlockSpec((rows, 4 * wide), lambda n, m, k: (0, 0)),
        ),
        out_shape=jax.ShapeDtypeStruct((rows, 4 * wide), jnp.bfloat16),
        compiler_params=params(32),
        cost_estimate=CHEAP,
    )(meta, count, *args)


def line_of_four(hidden, down_weight, adapter_shrink, adapter_expand, block_adapter, block_rows):
    rows, feat = hidden.shape
    adp, _, rank = adapter_shrink.shape
    p = lax.axis_index("pool")
    t = lax.axis_index("tensor")
    tensors = lax.axis_size("tensor")
    z, c = p // 2, p % 2
    outer = (z == 0) | (z == 3)

    def exchange(x):
        return lax.all_to_all(x, "tensor", split_axis=0, concat_axis=0, tiled=True)

    place = jnp.stack([jnp.where(outer, 0, 1), c, z]).astype(jnp.int32)

    mid = send(hidden, MIDDLE)
    partner = send(hidden, XOR[1])
    cuts = [(lo, min(lo + 2 * TILE, feat)) for lo in range(0, feat, 2 * TILE)]
    pieces = [down_weight[lo:hi] for lo, hi in cuts]
    others = [send(w, SIBLING) for w in pieces]
    weights = [(down_weight, lo // TILE, w, 0) for (lo, _), w in zip(cuts, others)]

    def whole(x):
        return [(x, lo // TILE, (hi - lo) // TILE, i) for i, (lo, hi) in enumerate(cuts)]

    shares = exchange(
        adapter_expand.transpose(0, 2, 1).reshape(adp, rank, tensors, SHARE).transpose(2, 0, 1, 3)
    ).reshape(tensors, adp * rank, SHARE)
    label = jnp.zeros((16, SHARE), jnp.bfloat16).at[0, : block_adapter.shape[0]].set(block_adapter.astype(jnp.bfloat16))
    j_own = products(place, [Rows(whole(hidden), None, 0)], weights, BLOCK)
    shares = after([j_own], shares)

    def shares_of(s):
        return lax.dynamic_index_in_dim(shares, z ^ s, 0, keepdims=False)

    told = [send(jnp.concatenate([shares_of(s), label], axis=0), XOR[s]) for s in (1, 2, 3)]

    ready = [partner, mid, *told]
    far = send(after(ready, partner), MIDDLE)
    out_mid = send(after(ready, mid), OUTWARD)
    shrink_w = adapter_shrink.transpose(0, 2, 1).reshape(adp * rank, feat)
    shrink_o = send(after(ready, shrink_w), INWARD)
    v_own = [send(after([shrink_o], w), INWARD) for w in pieces[NEAR // (2 * TILE) :]]
    r_own = exchange(j_own)
    j_partner = products(place, [Rows(whole(partner), None, 0)], weights, BLOCK)
    r_partner = exchange(j_partner)
    j_mid = products(place, [Rows(whole(after([j_partner], mid)), 1, 0)], weights, BLOCK)
    r_mid = exchange(j_mid)
    far_near = far[:, :NEAR]
    out_far = send(after([out_mid, shrink_o, j_partner], far_near), OUTWARD)
    j_third = products(
        place,
        [Rows(whole(after([r_partner, far_near], far)), 1, 0), Rows(whole(out_mid), 0, 0)],
        weights,
        BLOCK,
    )
    r_third = exchange(j_third)
    v_other = [send(after([j_third], w), SIBLING) for w in v_own]

    held = jnp.concatenate([shares_of(0)] + [x[: adp * rank] for x in told]).reshape(4 * adp, rank, SHARE)
    held = (held, send(held, SIBLING))
    names = [block_adapter] + [x[adp * rank, : block_adapter.shape[0]].astype(jnp.int32) for x in told]
    name_m = jnp.where(outer, names[2], names[3])
    name_f = jnp.where(outer, names[3], names[2])
    meta = jnp.concatenate([place, names[0], names[1], name_m, name_f])
    shrink_mine = jnp.concatenate([shrink_w, after([j_third], shrink_o)], axis=0)
    shrink_other = send(shrink_mine, SIBLING)
    sums = shrink_sums(meta, [[hidden], [mid], [partner], [far]], [0, 2, 1, 3], shrink_mine, shrink_other, held)
    r_sums = exchange(sums)
    low, swapped = low_sums(r_sums)
    low = add(low, send(swapped, MIDDLE))
    low_out = send(low, OUTWARD)

    rest = [(a, 0, b, 0) for a, b in zip(v_own, v_other)] + weights[: NEAR // (2 * TILE)]
    j_fifth = products(
        place,
        [
            Rows([(after([sums], far), NEAR // TILE, 2, 0), (far, NEAR // TILE + 2, 1, 1)], 1, 0),
            Rows([(out_far, 0, 2, 2), (out_far, 2, 2, 3)], 0, 0),
        ],
        rest,
        BLOCK,
    )
    r_fifth = exchange(j_fifth)

    def term(inner_slot, outer_slot):
        return (low, low_out, r_sums, (inner_slot, outer_slot))

    x_partner = finish(meta, None, r_partner, 0, term(1, 1))
    home_partner = send(x_partner, XOR[1])
    x_two = finish(meta, None, r_third, 0, term(3, 2))
    home_two = send(x_two, XOR[2])
    x_mid = finish(meta, 1, r_mid, 0, term(2, 2))
    home_mid = send(x_mid, MIDDLE)
    x_own = finish(meta, None, r_own, 0, term(0, 0))
    r_fifth = after([x_partner, x_two, x_mid, x_own], r_fifth)
    x_far = finish(meta, 0, r_fifth, 0, term(3, 3))
    to_far = send(x_far, INWARD)
    to_far = after([home_partner, home_two, home_mid], to_far)
    home_far = send(finish(meta, 1, r_fifth, 0, more=to_far), ACROSS)
    count = lax.dynamic_slice_in_dim(block_rows, t, 1, 0)
    return assemble(meta, count, x_own, home_partner, home_two, home_mid, home_far)


def solution(mesh):
    in_specs = (
        P("pool", "tensor"),
        P("tensor", "pool"),
        P("pool", "tensor", None),
        P("pool", "tensor", None),
        P("pool"),
        P("pool"),
    )
    out_specs = P(("pool", "tensor"), None)
    body = line_of_four if dict(mesh.shape) == {"pool": 8, "tensor": 4} else general
    return jax.shard_map(body, mesh=mesh, in_specs=in_specs, out_specs=out_specs, check_vma=False)
```

profile of v0, /device:TPU:0, one launch (start us, length us, event | category | flops | bytes accessed | tf_op | source)
XLA Modules:
  0.0 353.0 jit_solution(8608843980463646160)
XLA Ops:
  0.0 2.4 collective-permute-start.7
  2.4 4.1 %collective-permute-start.8 = (bf16[512,3584]{1,0:T(8,128)(2,1)}, bf16[512,3584]{1,0:T(8,128)(2,1)}, u32[]{:S(2)}, u32[]{:S(2)}) collective-permute-start(bf16[512,3584]{1,0:T(8,128)(2,1)} %refs_0_.3), channel_id=1, source_target_pairs={{0,8},{4,12},{8,0},{12,4},{16,24},{20,28},{24,16},{28,20},{1,9},{5... | collective-permute-start | bytes 11010056 | tf_op jit(solution)/shard_map/ppermute | solution.py:84
  6.6 2.3 slice.52
  8.9 5.8 %fusion.7 = (bf16[1024,1024]{1,0:T(8,128)(2,1)}, bf16[1024,1024]{1,0:T(8,128)(2,1)}, bf16[1024,1024]{1,0:T(8,128)(2,1)}) fusion(bf16[3584,1024]{1,0:T(8,128)(2,1)} %refs_10_.9), kind=kLoop, calls=%fused_computation.21 | loop fusion | bytes 12582912 | tf_op jit(solution)/shard_map/slice | solution.py:429
  15.7 2.2 reshape.50
  17.9 1.9 copy.11
  19.8 4.1 %all-to-all-start = ((bf16[4,2,64,512]{3,2,1,0:T(8,128)(2,1)}), bf16[4,2,64,512]{3,2,1,0:T(8,128)(2,1)}, u32[]{:S(2)}, u32[]{:S(2)}) async-start(bf16[4,2,64,512]{3,2,1,0:T(8,128)(2,1)} %copy.11), calls=%async_computation | async-start | bytes 1048576 | tf_op jit(solution)/shard_map/all_to_all | solution.py:422
  24.1 0.9 collective-permute-done.refs_5_.refs_9_
  25.3 15.6 %shard_map.64 = bf16[4,128,2048]{2,1,0:T(8,128)(2,1)} custom-call(s32[3]{0:T(128)S(1)} %pad_add_fusion.meta, bf16[512,3584]{1,0:T(8,128)(2,1)} %refs_0_.3, bf16[512,3584]{1,0:T(8,128)(2,1)} %refs_0_.3, bf16[512,3584]{1,0:T(8,128)(2,1)} %refs_0_.3, bf16[512,3584]{1,0:T(8,128)(2,1)} %refs_0_.3, bf16[3584,1024]{1,0:T(8,128)(2,1)} %refs_10_.9, ...), custom_call_target="tpu_custom_call" | custom-call | flops 1000 | bytes 1000 | tf_op jit(solution)/shard_map/pallas_call | solution.py:191
  40.9 4.5 %all-to-all-start.1 = ((bf16[4,128,2048]{2,1,0:T(8,128)(2,1)}), bf16[4,128,2048]{2,1,0:T(8,128)(2,1)}, u32[]{:S(2)}, u32[]{:S(2)}) async-start(bf16[4,128,2048]{2,1,0:T(8,128)(2,1)} %shard_map.64), calls=%async_computation.1 | async-start | bytes 4194304 | tf_op jit(solution)/shard_map/all_to_all | solution.py:422
  45.4 1.1 dynamic-slice_bitcast_fusion
  46.6 1.4 collective-permute-start.6
  48.0 0.7 collective-permute-start.4
  48.7 2.3 collective-permute-start.5
  51.0 40.5 %collective-permute-done.6 = bf16[144,512]{1,0:T(8,128)(2,1)S(1)} collective-permute-done((bf16[144,512]{1,0:T(8,128)(2,1)S(1)}, bf16[144,512]{1,0:T(8,128)(2,1)S(1)}, u32[]{:S(2)}, u32[]{:S(2)}) %collective-permute-start.6) | collective-permute-done | bytes 147488 | tf_op jit(solution)/shard_map/ppermute | solution.py:84
  91.5 1.5 collective-permute-done.4
  93.0 5.2 %collective-permute-done.5 = bf16[144,512]{1,0:T(8,128)(2,1)S(1)} collective-permute-done((bf16[144,512]{1,0:T(8,128)(2,1)S(1)}, bf16[144,512]{1,0:T(8,128)(2,1)S(1)}, u32[]{:S(2)}, u32[]{:S(2)}) %collective-permute-start.5) | collective-permute-done | bytes 147488 | tf_op jit(solution)/shard_map/ppermute | solution.py:84
  98.9 2.5 collective-permute-start.9
  101.4 1.3 collective-permute-start.10
  102.7 15.7 %shard_map.65 = bf16[4,128,2048]{2,1,0:T(8,128)(2,1)} custom-call(s32[3]{0:T(128)S(1)} %pad_add_fusion.meta, bf16[512,3584]{1,0:T(8,128)(2,1)} %collective-permute-done.8.refs_0_.refs_1_.refs_2_.refs_3_, bf16[512,3584]{1,0:T(8,128)(2,1)} %collective-permute-done.8.refs_0_.refs_1_.refs_2_.refs_3_, ...), custom_call_target="tpu_custom_call" | custom-call | flops 1000 | bytes 1000 | tf_op jit(solution)/shard_map/pallas_call | solution.py:191
  118.4 4.4 %all-to-all-start.2 = ((bf16[4,128,2048]{2,1,0:T(8,128)(2,1)}), bf16[4,128,2048]{2,1,0:T(8,128)(2,1)}, u32[]{:S(2)}, u32[]{:S(2)}) async-start(bf16[4,128,2048]{2,1,0:T(8,128)(2,1)} %shard_map.65), calls=%async_computation.2 | async-start | bytes 4194304 | tf_op jit(solution)/shard_map/all_to_all | solution.py:422
  122.9 7.3 %collective-permute-start.11 = (bf16[128,3584]{1,0:T(8,128)(2,1)}, bf16[128,3584]{1,0:T(8,128)(2,1)}, u32[]{:S(2)}, u32[]{:S(2)}) collective-permute-start(bf16[128,3584]{1,0:T(8,128)(2,1)} %bitcast.32), channel_id=1, source_target_pairs={{0,8},{4,12},{24,16},{28,20},{1,9},{5,13},{25,17},{29,21},{2,10},{... | collective-permute-start | bytes 2752520 | tf_op jit(solution)/shard_map/ppermute | solution.py:84
  130.2 17.8 %collective-permute-done.11 = bf16[128,3584]{1,0:T(8,128)(2,1)} collective-permute-done((bf16[128,3584]{1,0:T(8,128)(2,1)}, bf16[128,3584]{1,0:T(8,128)(2,1)}, u32[]{:S(2)}, u32[]{:S(2)}) %collective-permute-start.11) | collective-permute-done | bytes 917536 | tf_op jit(solution)/shard_map/ppermute | solution.py:84
  148.0 5.7 %collective-permute-start.20 = (bf16[1024,1024]{1,0:T(8,128)(2,1)}, bf16[1024,1024]{1,0:T(8,128)(2,1)}, u32[]{:S(2)}, u32[]{:S(2)}) collective-permute-start(bf16[1024,1024]{1,0:T(8,128)(2,1)} %get-tuple-element.45), channel_id=1, source_target_pairs={{0,8},{4,12},{24,16},{28,20},{1,9},{5,13},{25,17},{29,21},{2,10},{... | collective-permute-start | bytes 6291464 | tf_op jit(solution)/shard_map/ppermute | solution.py:84
  153.7 5.3 %shard_map.73 = bf16[4,128,2048]{2,1,0:T(8,128)(2,1)} custom-call(s32[3]{0:T(128)S(1)} %pad_add_fusion.meta, bf16[512,3584]{1,0:T(8,128)(2,1)} %collective-permute-done.7.refs_1_.refs_0_.refs_2_.refs_3_, bf16[512,3584]{1,0:T(8,128)(2,1)} %collective-permute-done.7.refs_1_.refs_0_.refs_2_.refs_3_, ...), custom_call_target="tpu_custom_call" | custom-call | flops 1000 | bytes 1000 | tf_op jit(solution)/shard_map/pallas_call | solution.py:191
  159.1 4.5 %all-to-all-start.5 = ((bf16[4,128,2048]{2,1,0:T(8,128)(2,1)}), bf16[4,128,2048]{2,1,0:T(8,128)(2,1)}, u32[]{:S(2)}, u32[]{:S(2)}) async-start(bf16[4,128,2048]{2,1,0:T(8,128)(2,1)} %shard_map.73), calls=%async_computation.5 | async-start | bytes 4194304 | tf_op jit(solution)/shard_map/all_to_all | solution.py:422
  163.5 3.1 slice.63
  166.7 17.2 %collective-permute-done.10.refs_4_.refs_5_.refs_6_.refs_7_ = bf16[512,3584]{1,0:T(8,128)(2,1)} collective-permute-done((bf16[512,3584]{1,0:T(8,128)(2,1)}, bf16[512,3584]{1,0:T(8,128)(2,1)}, u32[]{:S(2)}, u32[]{:S(2)}) %collective-permute-start.10) | collective-permute-done | bytes 3670048 | tf_op jit(solution)/shard_map/ppermute | solution.py:84
  183.9 16.7 %shard_map.66 = bf16[4,128,2048]{2,1,0:T(8,128)(2,1)} custom-call(s32[3]{0:T(128)S(1)} %pad_add_fusion.meta, bf16[512,3584]{1,0:T(8,128)(2,1)} %collective-permute-done.9.refs_0_.refs_1_.refs_2_.refs_3_, bf16[512,3584]{1,0:T(8,128)(2,1)} %collective-permute-done.9.refs_0_.refs_1_.refs_2_.refs_3_, ...), custom_call_target="tpu_custom_call" | custom-call | flops 1000 | bytes 1000 | tf_op jit(solution)/shard_map/pallas_call | solution.py:191
  200.6 2.6 pad_maximum_fusion.refs_4_
  203.2 3.9 %all-to-all-start.4 = ((bf16[4,128,2048]{2,1,0:T(8,128)(2,1)}), bf16[4,128,2048]{2,1,0:T(8,128)(2,1)S(1)}, u32[]{:S(2)}, u32[]{:S(2)}) async-start(bf16[4,128,2048]{2,1,0:T(8,128)(2,1)} %shard_map.66), calls=%async_computation.4 | async-start | bytes 4194304 | tf_op jit(solution)/shard_map/all_to_all | solution.py:422
  207.2 3.2 collective-permute-start.22
  210.3 1.3 collective-permute-start.19
  212.4 0.7 fusion.5
  213.1 19.3 %collective-permute-done.22.refs_6_ = bf16[512,1024]{1,0:T(8,128)(2,1)} collective-permute-done((bf16[512,1024]{1,0:T(8,128)(2,1)}, bf16[512,1024]{1,0:T(8,128)(2,1)}, u32[]{:S(2)}, u32[]{:S(2)}) %collective-permute-start.22) | collective-permute-done | bytes 1048608 | tf_op jit(solution)/shard_map/ppermute | solution.py:84
  233.2 2.0 copy-done
  235.2 4.0 %shard_map.67 = bf16[4,128,1280]{2,1,0:T(8,128)(2,1)} custom-call(s32[19]{0:T(128)S(1)} %concatenate.24.meta, bf16[512,3584]{1,0:T(8,128)(2,1)S(1)} %copy-done, bf16[512,3584]{1,0:T(8,128)(2,1)} %collective-permute-done.7.refs_1_.refs_0_.refs_2_.refs_3_, bf16[512,3584]{1,0:T(8,128)(2,1)} %collective-permute-done.8.refs_0_.refs_1_.refs_2_.refs_3_, ...), custom_call_target="tpu_custom_call" | custom-call | flops 1000 | bytes 1000 | tf_op jit(solution)/shard_map/pallas_call | solution.py:264
  239.2 1.3 copy-done.4
  240.6 3.9 %all-to-all-start.3 = ((bf16[4,128,1280]{2,1,0:T(8,128)(2,1)}), bf16[4,128,1280]{2,1,0:T(8,128)(2,1)S(1)}, u32[]{:S(2)}, u32[]{:S(2)}) async-start(bf16[4,128,1280]{2,1,0:T(8,128)(2,1)} %shard_map.67), calls=%async_computation.3 | async-start | bytes 2621440 | tf_op jit(solution)/shard_map/all_to_all | solution.py:422
  244.4 15.5 %collective-permute-done.19.refs_2_.refs_3_ = bf16[512,2048]{1,0:T(8,128)(2,1)} collective-permute-done((bf16[512,2048]{1,0:T(8,128)(2,1)}, bf16[512,2048]{1,0:T(8,128)(2,1)}, u32[]{:S(2)}, u32[]{:S(2)}) %collective-permute-start.19) | collective-permute-done | bytes 2097184 | tf_op jit(solution)/shard_map/ppermute | solution.py:84
  260.0 12.0 %shard_map.75 = bf16[4,128,2048]{2,1,0:T(8,128)(2,1)} custom-call(s32[3]{0:T(128)S(1)} %pad_add_fusion.meta, bf16[512,3584]{1,0:T(8,128)(2,1)} %collective-permute-done.9.refs_0_.refs_1_.refs_2_.refs_3_, bf16[512,3584]{1,0:T(8,128)(2,1)} %collective-permute-done.9.refs_0_.refs_1_.refs_2_.refs_3_, bf16[512,2048]{1,0:T(8,128)(2,1)} %collective-permute-done.19.refs_2_.refs_3_, ...), custom_call_target="tpu_custom_call" | custom-call | flops 1000 | bytes 1000 | tf_op jit(solution)/shard_map/pallas_call | solution.py:191
  272.0 1.1 copy-done.1
  273.1 3.9 %all-to-all-start.6 = ((bf16[4,128,2048]{2,1,0:T(8,128)(2,1)}), bf16[4,128,2048]{2,1,0:T(8,128)(2,1)S(1)}, u32[]{:S(2)}, u32[]{:S(2)}) async-start(bf16[4,128,2048]{2,1,0:T(8,128)(2,1)} %shard_map.75), calls=%async_computation.6 | async-start | bytes 4194304 | tf_op jit(solution)/shard_map/all_to_all | solution.py:422
  277.0 1.8 shard_map.68
  280.0 1.5 shard_map.69.refs_1_
  281.6 1.4 collective-permute-start.15
  283.0 11.0 %collective-permute-done.15.refs_2_ = bf16[128,256]{1,0:T(8,128)(2,1)S(1)} collective-permute-done((bf16[128,256]{1,0:T(8,128)(2,1)}, bf16[128,256]{1,0:T(8,128)(2,1)S(1)}, u32[]{:S(2)}, u32[]{:S(2)}) %collective-permute-start.15) | collective-permute-done | bytes 65568 | tf_op jit(solution)/shard_map/ppermute | solution.py:84
  293.9 0.8 copy-done.6
  294.8 3.0 shard_map.71
  297.8 2.1 shard_map.72
  300.0 2.4 collective-permute-start.17
  302.4 2.8 shard_map.74
  305.2 1.6 collective-permute-start.18
  306.8 2.4 shard_map.70.own
  309.2 0.8 copy-done.8
  310.0 1.4 shard_map.76
  311.4 3.3 collective-permute-start.24
  314.7 3.5 collective-permute-done.16.one
  318.2 9.0 %collective-permute-done.17.two = bf16[128,2048]{1,0:T(8,128)(2,1)} collective-permute-done((bf16[128,2048]{1,0:T(8,128)(2,1)}, bf16[128,2048]{1,0:T(8,128)(2,1)}, u32[]{:S(2)}, u32[]{:S(2)}) %collective-permute-start.17) | collective-permute-done | bytes 524320 | tf_op jit(solution)/shard_map/ppermute | solution.py:84
  327.3 2.9 collective-permute-done.24.refs_1_
  330.2 1.6 shard_map.77
  331.7 1.3 collective-permute-start.25
  333.6 15.3 %collective-permute-done.25.outer_three = bf16[128,2048]{1,0:T(8,128)(2,1)S(1)} collective-permute-done((bf16[128,2048]{1,0:T(8,128)(2,1)}, bf16[128,2048]{1,0:T(8,128)(2,1)S(1)}, u32[]{:S(2)}, u32[]{:S(2)}) %collective-permute-start.25) | collective-permute-done | bytes 524320 | tf_op jit(solution)/shard_map/ppermute | solution.py:84
  348.9 4.1 %shard_map.78 = bf16[128,8192]{1,0:T(8,128)(2,1)} custom-call(s32[19]{0:T(128)S(1)} %concatenate.24.meta, s32[1]{0:T(128)} %dynamic_slice.19.count, bf16[128,2048]{1,0:T(8,128)(2,1)S(1)} %copy-done.9, bf16[128,2048]{1,0:T(8,128)(2,1)} %collective-permute-done.16.one, bf16[128,2048]{1,0:T(8,128)(2,1)} %collective-permute-done.17.two, ...), custom_call_target="tpu_custom_call" | custom-call | flops 1000 | bytes 1000 | tf_op jit(solution)/shard_map/pallas_call | solution.py:398
  (74 shorter events, 5.5 us)
Async XLA Ops:
  0.0 98.9 %collective-permute-start.7 = (bf16[512,3584]{1,0:T(8,128)(2,1)}, bf16[512,3584]{1,0:T(8,128)(2,1)}, u32[]{:S(2)}, u32[]{:S(2)}) collective-permute-start(bf16[512,3584]{1,0:T(8,128)(2,1)} %refs_0_.3), channel_id=1, source_target_pairs={{8,16},{12,20},{16,8},{20,12},{9,17},{13,21},{17,9},{21,13},{10,18... | collective-permute-start | bytes 11010056 | tf_op jit(solution)/shard_map/ppermute | solution.py:84
  2.4 96.5 %collective-permute-start.8 = (bf16[512,3584]{1,0:T(8,128)(2,1)}, bf16[512,3584]{1,0:T(8,128)(2,1)}, u32[]{:S(2)}, u32[]{:S(2)}) collective-permute-start(bf16[512,3584]{1,0:T(8,128)(2,1)} %refs_0_.3), channel_id=1, source_target_pairs={{0,8},{4,12},{8,0},{12,4},{16,24},{20,28},{24,16},{28,20},{1,9},{5... | collective-permute-start | bytes 11010056 | tf_op jit(solution)/shard_map/ppermute | solution.py:84
  8.9 6.3 %collective-permute-start.3 = (bf16[512,1024]{1,0:T(8,128)(2,1)}, bf16[512,1024]{1,0:T(8,128)(2,1)S(1)}, u32[]{:S(2)}, u32[]{:S(2)}) collective-permute-start(bf16[512,1024]{1,0:T(8,128)(2,1)} %slice.52), channel_id=1, source_target_pairs={{0,4},{4,0},{8,12},{12,8},{16,20},{20,16},{24,28},{28,24},{1,5},{5... | collective-permute-start | bytes 3145736 | tf_op jit(solution)/shard_map/ppermute | solution.py:84
  14.7 9.4 %copy-start.17 = (s32[4]{0:T(128)S(1)}, s32[4]{0:T(128)}, u32[]{:S(2)}) copy-start(s32[4]{0:T(128)} %param.12) | copy-start | bytes 52
  14.7 9.4 %collective-permute-start.1 = (bf16[1024,1024]{1,0:T(8,128)(2,1)}, bf16[1024,1024]{1,0:T(8,128)(2,1)}, u32[]{:S(2)}, u32[]{:S(2)}) collective-permute-start(bf16[1024,1024]{1,0:T(8,128)(2,1)} %get-tuple-element.52), channel_id=1, source_target_pairs={{0,4},{4,0},{8,12},{12,8},{16,20},{20,16},{24,28},{28,24},{1,5},{5... | collective-permute-start | bytes 6291464 | tf_op jit(solution)/shard_map/ppermute | solution.py:84
  15.2 9.9 %collective-permute-start = (bf16[1024,1024]{1,0:T(8,128)(2,1)}, bf16[1024,1024]{1,0:T(8,128)(2,1)S(1)}, u32[]{:S(2)}, u32[]{:S(2)}) collective-permute-start(bf16[1024,1024]{1,0:T(8,128)(2,1)} %get-tuple-element.53), channel_id=1, source_target_pairs={{0,4},{4,0},{8,12},{12,8},{16,20},{20,16},{24,28},{28,24},{1,5},{5... | collective-permute-start | bytes 6291464 | tf_op jit(solution)/shard_map/ppermute | solution.py:84
  15.2 10.1 %collective-permute-start.2 = (bf16[1024,1024]{1,0:T(8,128)(2,1)}, bf16[1024,1024]{1,0:T(8,128)(2,1)}, u32[]{:S(2)}, u32[]{:S(2)}) collective-permute-start(bf16[1024,1024]{1,0:T(8,128)(2,1)} %get-tuple-element.45), channel_id=1, source_target_pairs={{0,4},{4,0},{8,12},{12,8},{16,20},{20,16},{24,28},{28,24},{1,5},{5... | collective-permute-start | bytes 6291464 | tf_op jit(solution)/shard_map/ppermute | solution.py:84
  19.8 21.1 %all-to-all-start = ((bf16[4,2,64,512]{3,2,1,0:T(8,128)(2,1)}), bf16[4,2,64,512]{3,2,1,0:T(8,128)(2,1)}, u32[]{:S(2)}, u32[]{:S(2)}) async-start(bf16[4,2,64,512]{3,2,1,0:T(8,128)(2,1)} %copy.11), calls=%async_computation | async-start | bytes 1048576 | tf_op jit(solution)/shard_map/all_to_all | solution.py:422
  25.0 158.8 %copy-start.3 = (bf16[1024,1024]{1,0:T(8,128)(2,1)}, bf16[1024,1024]{1,0:T(8,128)(2,1)S(1)}, u32[]{:S(2)}) copy-start(bf16[1024,1024]{1,0:T(8,128)(2,1)S(1)} %collective-permute-done.refs_5_.refs_9_) | copy-start | bytes 6291460
  40.9 77.5 %all-to-all-start.1 = ((bf16[4,128,2048]{2,1,0:T(8,128)(2,1)}), bf16[4,128,2048]{2,1,0:T(8,128)(2,1)}, u32[]{:S(2)}, u32[]{:S(2)}) async-start(bf16[4,128,2048]{2,1,0:T(8,128)(2,1)} %shard_map.64), calls=%async_computation.1 | async-start | bytes 4194304 | tf_op jit(solution)/shard_map/all_to_all | solution.py:422
  46.6 45.0 %collective-permute-start.6 = (bf16[144,512]{1,0:T(8,128)(2,1)S(1)}, bf16[144,512]{1,0:T(8,128)(2,1)S(1)}, u32[]{:S(2)}, u32[]{:S(2)}) collective-permute-start(bf16[144,512]{1,0:T(8,128)(2,1)S(1)} %get-tuple-element.60), channel_id=1, source_target_pairs={{0,24},{4,28},{8,16},{12,20},{16,8},{20,12},{24,0},{28,4},{1,25},{... | collective-permute-start | bytes 442376 | tf_op jit(solution)/shard_map/ppermute | solution.py:84
  48.0 45.0 %collective-permute-start.4 = (bf16[144,512]{1,0:T(8,128)(2,1)S(1)}, bf16[144,512]{1,0:T(8,128)(2,1)S(1)}, u32[]{:S(2)}, u32[]{:S(2)}) collective-permute-start(bf16[144,512]{1,0:T(8,128)(2,1)S(1)} %get-tuple-element.61), channel_id=1, source_target_pairs={{0,8},{4,12},{8,0},{12,4},{16,24},{20,28},{24,16},{28,20},{1,9},{5... | collective-permute-start | bytes 442376 | tf_op jit(solution)/shard_map/ppermute | solution.py:84
  48.7 49.6 %collective-permute-start.5 = (bf16[144,512]{1,0:T(8,128)(2,1)S(1)}, bf16[144,512]{1,0:T(8,128)(2,1)S(1)}, u32[]{:S(2)}, u32[]{:S(2)}) collective-permute-start(bf16[144,512]{1,0:T(8,128)(2,1)S(1)} %get-tuple-element.62), channel_id=1, source_target_pairs={{0,16},{4,20},{8,24},{12,28},{16,0},{20,4},{24,8},{28,12},{1,17},{... | collective-permute-start | bytes 442376 | tf_op jit(solution)/shard_map/ppermute | solution.py:84
  91.5 26.9 %copy-start.11 = (bf16[144,512]{1,0:T(8,128)(2,1)}, bf16[144,512]{1,0:T(8,128)(2,1)S(1)}, u32[]{:S(2)}) copy-start(bf16[144,512]{1,0:T(8,128)(2,1)S(1)} %collective-permute-done.6) | copy-start | bytes 442372
  93.0 5.9 %copy-start.14 = (bf16[144,512]{1,0:T(8,128)(2,1)}, bf16[144,512]{1,0:T(8,128)(2,1)S(1)}, u32[]{:S(2)}) copy-start(bf16[144,512]{1,0:T(8,128)(2,1)S(1)} %collective-permute-done.4) | copy-start | bytes 442372
  98.3 0.6 copy-start.12
  98.9 64.6 %collective-permute-start.9 = (bf16[512,3584]{1,0:T(8,128)(2,1)}, bf16[512,3584]{1,0:T(8,128)(2,1)}, u32[]{:S(2)}, u32[]{:S(2)}) collective-permute-start(bf16[512,3584]{1,0:T(8,128)(2,1)} %collective-permute-done.8.refs_0_.refs_1_.refs_2_.refs_3_), channel_id=1, source_target_pairs={{8,16},{12,20},{16,8},{20,12},{9,17},{13,21},{17,9},{21,13},{10,18... | collective-permute-start | bytes 11010056 | tf_op jit(solution)/shard_map/ppermute | solution.py:84
  101.4 82.4 %collective-permute-start.10 = (bf16[512,3584]{1,0:T(8,128)(2,1)}, bf16[512,3584]{1,0:T(8,128)(2,1)}, u32[]{:S(2)}, u32[]{:S(2)}) collective-permute-start(bf16[512,3584]{1,0:T(8,128)(2,1)} %collective-permute-done.7.refs_1_.refs_0_.refs_2_.refs_3_), channel_id=1, source_target_pairs={{8,0},{12,4},{16,24},{20,28},{9,1},{13,5},{17,25},{21,29},{10,2},{... | collective-permute-start | bytes 11010056 | tf_op jit(solution)/shard_map/ppermute | solution.py:84
  118.4 40.6 %all-to-all-start.2 = ((bf16[4,128,2048]{2,1,0:T(8,128)(2,1)}), bf16[4,128,2048]{2,1,0:T(8,128)(2,1)}, u32[]{:S(2)}, u32[]{:S(2)}) async-start(bf16[4,128,2048]{2,1,0:T(8,128)(2,1)} %shard_map.65), calls=%async_computation.2 | async-start | bytes 4194304 | tf_op jit(solution)/shard_map/all_to_all | solution.py:422
  122.9 25.1 %collective-permute-start.11 = (bf16[128,3584]{1,0:T(8,128)(2,1)}, bf16[128,3584]{1,0:T(8,128)(2,1)}, u32[]{:S(2)}, u32[]{:S(2)}) collective-permute-start(bf16[128,3584]{1,0:T(8,128)(2,1)} %bitcast.32), channel_id=1, source_target_pairs={{0,8},{4,12},{24,16},{28,20},{1,9},{5,13},{25,17},{29,21},{2,10},{... | collective-permute-start | bytes 2752520 | tf_op jit(solution)/shard_map/ppermute | solution.py:84
  148.0 62.3 %collective-permute-start.20 = (bf16[1024,1024]{1,0:T(8,128)(2,1)}, bf16[1024,1024]{1,0:T(8,128)(2,1)}, u32[]{:S(2)}, u32[]{:S(2)}) collective-permute-start(bf16[1024,1024]{1,0:T(8,128)(2,1)} %get-tuple-element.45), channel_id=1, source_target_pairs={{0,8},{4,12},{24,16},{28,20},{1,9},{5,13},{25,17},{29,21},{2,10},{... | collective-permute-start | bytes 6291464 | tf_op jit(solution)/shard_map/ppermute | solution.py:84
  159.1 44.1 %all-to-all-start.5 = ((bf16[4,128,2048]{2,1,0:T(8,128)(2,1)}), bf16[4,128,2048]{2,1,0:T(8,128)(2,1)}, u32[]{:S(2)}, u32[]{:S(2)}) async-start(bf16[4,128,2048]{2,1,0:T(8,128)(2,1)} %shard_map.73), calls=%async_computation.5 | async-start | bytes 4194304 | tf_op jit(solution)/shard_map/all_to_all | solution.py:422
  166.7 33.9 %copy-start.10 = (bf16[2,3584,64]{1,2,0:T(8,128)(2,1)S(1)}, bf16[2,3584,64]{1,2,0:T(8,128)(2,1)}, u32[]{:S(2)}) copy-start(bf16[2,3584,64]{1,2,0:T(8,128)(2,1)} %param.10) | copy-start | bytes 2752516
  203.2 8.5 %copy-start.15 = (bf16[144,512]{1,0:T(8,128)(2,1)S(1)}, bf16[144,512]{1,0:T(8,128)(2,1)}, u32[]{:S(2)}) copy-start(bf16[144,512]{1,0:T(8,128)(2,1)} %copy-done.14) | copy-start | bytes 442372
  203.2 8.6 %copy-start.13 = (bf16[144,512]{1,0:T(8,128)(2,1)S(1)}, bf16[144,512]{1,0:T(8,128)(2,1)}, u32[]{:S(2)}) copy-start(bf16[144,512]{1,0:T(8,128)(2,1)} %copy-done.12) | copy-start | bytes 442372
  203.2 8.6 %slice-start = ((bf16[144,512]{1,0:T(8,128)(2,1)}), bf16[128,512]{1,0:T(8,128)(2,1)S(1)}, s32[]{:S(2)}) async-start(bf16[144,512]{1,0:T(8,128)(2,1)} %copy-done.11), calls=%async_computation.7 | async-start | bytes 262144 | tf_op jit(solution)/shard_map/slice | solution.py:470
  203.2 30.0 %collective-permute-start.12 = (bf16[256,3584]{1,0:T(8,128)(2,1)}, bf16[256,3584]{1,0:T(8,128)(2,1)}, u32[]{:S(2)}, u32[]{:S(2)}) collective-permute-start(bf16[256,3584]{1,0:T(8,128)(2,1)} %pad_maximum_fusion.refs_4_), channel_id=1, source_target_pairs={{0,4},{4,0},{8,12},{12,8},{16,20},{20,16},{24,28},{28,24},{1,5},{5... | collective-permute-start | bytes 5505032 | tf_op jit(solution)/shard_map/ppermute | solution.py:84
  203.2 36.0 %all-to-all-start.4 = ((bf16[4,128,2048]{2,1,0:T(8,128)(2,1)}), bf16[4,128,2048]{2,1,0:T(8,128)(2,1)S(1)}, u32[]{:S(2)}, u32[]{:S(2)}) async-start(bf16[4,128,2048]{2,1,0:T(8,128)(2,1)} %shard_map.66), calls=%async_computation.4 | async-start | bytes 4194304 | tf_op jit(solution)/shard_map/all_to_all | solution.py:422
  207.2 25.3 %collective-permute-start.22 = (bf16[512,1024]{1,0:T(8,128)(2,1)}, bf16[512,1024]{1,0:T(8,128)(2,1)}, u32[]{:S(2)}, u32[]{:S(2)}) collective-permute-start(bf16[512,1024]{1,0:T(8,128)(2,1)} %slice.52), channel_id=1, source_target_pairs={{0,8},{4,12},{24,16},{28,20},{1,9},{5,13},{25,17},{29,21},{2,10},{... | collective-permute-start | bytes 3145736 | tf_op jit(solution)/shard_map/ppermute | solution.py:84
  210.3 49.6 %collective-permute-start.19 = (bf16[512,2048]{1,0:T(8,128)(2,1)}, bf16[512,2048]{1,0:T(8,128)(2,1)}, u32[]{:S(2)}, u32[]{:S(2)}) collective-permute-start(bf16[512,2048]{1,0:T(8,128)(2,1)} %slice.63), channel_id=1, source_target_pairs={{8,0},{12,4},{16,24},{20,28},{9,1},{13,5},{17,25},{21,29},{10,2},{... | collective-permute-start | bytes 6291464 | tf_op jit(solution)/shard_map/ppermute | solution.py:84
  211.6 48.3 %collective-permute-start.21 = (bf16[1024,1024]{1,0:T(8,128)(2,1)}, bf16[1024,1024]{1,0:T(8,128)(2,1)}, u32[]{:S(2)}, u32[]{:S(2)}) collective-permute-start(bf16[1024,1024]{1,0:T(8,128)(2,1)} %collective-permute-done.20.refs_4_), channel_id=1, source_target_pairs={{0,4},{4,0},{8,12},{12,8},{16,20},{20,16},{24,28},{28,24},{1,5},{5... | collective-permute-start | bytes 6291464 | tf_op jit(solution)/shard_map/ppermute | solution.py:84
  211.8 21.3 %collective-permute-start.13 = (bf16[8,64,512]{2,1,0:T(8,128)(2,1)S(1)}, bf16[8,64,512]{2,1,0:T(8,128)(2,1)S(1)}, u32[]{:S(2)}, u32[]{:S(2)}) collective-permute-start(bf16[8,64,512]{2,1,0:T(8,128)(2,1)S(1)} %bitcast.29), channel_id=1, source_target_pairs={{0,4},{4,0},{8,12},{12,8},{16,20},{20,16},{24,28},{28,24},{1,5},{5... | collective-permute-start | bytes 1572872 | tf_op jit(solution)/shard_map/ppermute | solution.py:84
  232.4 12.0 %collective-permute-start.23 = (bf16[512,1024]{1,0:T(8,128)(2,1)}, bf16[512,1024]{1,0:T(8,128)(2,1)}, u32[]{:S(2)}, u32[]{:S(2)}) collective-permute-start(bf16[512,1024]{1,0:T(8,128)(2,1)} %collective-permute-done.22.refs_6_), channel_id=1, source_target_pairs={{0,4},{4,0},{8,12},{12,8},{16,20},{20,16},{24,28},{28,24},{1,5},{5... | collective-permute-start | bytes 3145736 | tf_op jit(solution)/shard_map/ppermute | solution.py:84
  233.2 2.0 copy-start
  239.2 1.3 copy-start.4
  240.6 31.5 %all-to-all-start.3 = ((bf16[4,128,1280]{2,1,0:T(8,128)(2,1)}), bf16[4,128,1280]{2,1,0:T(8,128)(2,1)S(1)}, u32[]{:S(2)}, u32[]{:S(2)}) async-start(bf16[4,128,1280]{2,1,0:T(8,128)(2,1)} %shard_map.67), calls=%async_computation.3 | async-start | bytes 2621440 | tf_op jit(solution)/shard_map/all_to_all | solution.py:422
  272.0 1.1 copy-start.1
  273.1 36.9 %all-to-all-start.6 = ((bf16[4,128,2048]{2,1,0:T(8,128)(2,1)}), bf16[4,128,2048]{2,1,0:T(8,128)(2,1)S(1)}, u32[]{:S(2)}, u32[]{:S(2)}) async-start(bf16[4,128,2048]{2,1,0:T(8,128)(2,1)} %shard_map.75), calls=%async_computation.6 | async-start | bytes 4194304 | tf_op jit(solution)/shard_map/all_to_all | solution.py:422
  277.0 17.0 %copy-start.2 = (bf16[4,128,1280]{2,1,0:T(8,128)(2,1)S(1)}, bf16[4,128,1280]{2,1,0:T(8,128)(2,1)}, u32[]{:S(2)}) copy-start(bf16[4,128,1280]{2,1,0:T(8,128)(2,1)} %copy-done.1) | copy-start | bytes 3932164
  278.8 0.7 collective-permute-start.14
  279.4 0.6 copy-start.16
  281.6 16.3 %copy-start.5 = (bf16[4,128,2048]{2,1,0:T(8,128)(2,1)S(1)}, bf16[4,128,2048]{2,1,0:T(8,128)(2,1)}, u32[]{:S(2)}) copy-start(bf16[4,128,2048]{2,1,0:T(8,128)(2,1)} %copy-done.4) | copy-start | bytes 6291460
  281.6 12.4 %collective-permute-start.15 = (bf16[128,256]{1,0:T(8,128)(2,1)}, bf16[128,256]{1,0:T(8,128)(2,1)S(1)}, u32[]{:S(2)}, u32[]{:S(2)}) collective-permute-start(bf16[128,256]{1,0:T(8,128)(2,1)} %shard_map.69.refs_1_), channel_id=1, source_target_pairs={{8,0},{12,4},{16,24},{20,28},{9,1},{13,5},{17,25},{21,29},{10,2},{... | collective-permute-start | bytes 196616 | tf_op jit(solution)/shard_map/ppermute | solution.py:84
  293.9 0.8 copy-start.6
  297.8 20.4 %collective-permute-start.16 = (bf16[128,2048]{1,0:T(8,128)(2,1)}, bf16[128,2048]{1,0:T(8,128)(2,1)}, u32[]{:S(2)}, u32[]{:S(2)}) collective-permute-start(bf16[128,2048]{1,0:T(8,128)(2,1)} %shard_map.71), channel_id=1, source_target_pairs={{0,8},{4,12},{8,0},{12,4},{16,24},{20,28},{24,16},{28,20},{1,9},{5... | collective-permute-start | bytes 1572872 | tf_op jit(solution)/shard_map/ppermute | solution.py:84
  300.0 27.3 %collective-permute-start.17 = (bf16[128,2048]{1,0:T(8,128)(2,1)}, bf16[128,2048]{1,0:T(8,128)(2,1)}, u32[]{:S(2)}, u32[]{:S(2)}) collective-permute-start(bf16[128,2048]{1,0:T(8,128)(2,1)} %shard_map.72), channel_id=1, source_target_pairs={{0,16},{4,20},{8,24},{12,28},{16,0},{20,4},{24,8},{28,12},{1,17},{... | collective-permute-start | bytes 1572872 | tf_op jit(solution)/shard_map/ppermute | solution.py:84
  305.2 4.8 %copy-start.7 = (bf16[128,256]{1,0:T(8,128)(2,1)S(1)}, bf16[128,256]{1,0:T(8,128)(2,1)}, u32[]{:S(2)}) copy-start(bf16[128,256]{1,0:T(8,128)(2,1)} %shard_map.69.refs_1_) | copy-start | bytes 196612
  305.2 22.1 %collective-permute-start.18 = (bf16[128,2048]{1,0:T(8,128)(2,1)}, bf16[128,2048]{1,0:T(8,128)(2,1)}, u32[]{:S(2)}, u32[]{:S(2)}) collective-permute-start(bf16[128,2048]{1,0:T(8,128)(2,1)} %shard_map.74), channel_id=1, source_target_pairs={{8,16},{12,20},{16,8},{20,12},{9,17},{13,21},{17,9},{21,13},{10,18... | collective-permute-start | bytes 1572872 | tf_op jit(solution)/shard_map/ppermute | solution.py:84
  309.2 0.8 copy-start.8
  311.4 21.6 %copy-start.18 = (s32[4]{0:T(128)S(1)}, s32[4]{0:T(128)}, u32[]{:S(2)}) copy-start(s32[4]{0:T(128)} %param.13) | copy-start | bytes 52
  311.4 37.5 %copy-start.9 = (bf16[128,2048]{1,0:T(8,128)(2,1)S(1)}, bf16[128,2048]{1,0:T(8,128)(2,1)}, u32[]{:S(2)}) copy-start(bf16[128,2048]{1,0:T(8,128)(2,1)} %copy-done.8) | copy-start | bytes 1572868
  311.4 18.7 %collective-permute-start.24 = (bf16[128,2048]{1,0:T(8,128)(2,1)S(1)}, bf16[128,2048]{1,0:T(8,128)(2,1)S(1)}, u32[]{:S(2)}, u32[]{:S(2)}) collective-permute-start(bf16[128,2048]{1,0:T(8,128)(2,1)S(1)} %shard_map.76), channel_id=1, source_target_pairs={{0,8},{4,12},{24,16},{28,20},{1,9},{5,13},{25,17},{29,21},{2,10},{... | collective-permute-start | bytes 1572872 | tf_op jit(solution)/shard_map/ppermute | solution.py:84
  331.7 17.2 %collective-permute-start.25 = (bf16[128,2048]{1,0:T(8,128)(2,1)}, bf16[128,2048]{1,0:T(8,128)(2,1)S(1)}, u32[]{:S(2)}, u32[]{:S(2)}) collective-permute-start(bf16[128,2048]{1,0:T(8,128)(2,1)} %shard_map.77), channel_id=1, source_target_pairs={{8,24},{12,28},{16,0},{20,4},{9,25},{13,29},{17,1},{21,5},{10,26},... | collective-permute-start | bytes 1572872 | tf_op jit(solution)/shard_map/ppermute | solution.py:84
where the time goes:
time: 355 us; the launch traced here: 353 us
  waiting for transfers between devices  160 us (45%)
  Pallas kernels  90.1 us (25%)
  starting transfers between devices  73.8 us (21%)
  local copies, waits for them, and re-layouts  24.6 us (7%)
  other arithmetic  4.14 us (1%)
    ppermute x26, waiting for transfers between devices, send(): return lax.ppermute(x, 'pool', pairs)  160 us
    pallas_call x5, Pallas kernels, products(): pl.pallas_call(functools.partial(products_kernel, jobs, len(weights)), gr...  65.3 us
    ppermute x26, starting transfers between devices, send(): return lax.ppermute(x, 'pool', pairs)  44.6 us
    all_to_all x7, starting transfers between devices, exchange(): return lax.all_to_all(x, 'tensor', split_axis=0, concat_axis=0, tiled=True)  29.2 us
    pallas_call x6, Pallas kernels, finish(): pl.pallas_call(functools.partial(finish_kernel, role, row, rows, lanes, m...  13.3 us
    slice x2, local copies, waits for them, and re-layouts, line_of_four(): pieces = [down_weight[lo:hi] for lo, hi in cuts]  8.07 us
    unnamed x38, local copies, waits for them, and re-layouts  7.35 us
  transfers between devices with their start and end apart: 33, of which 14 were waited for; matrix products, arithmetic and copies ran while one was open for 6% of the time, Pallas kernels for 24%

commit v1 on v0

--- a/solution.py
+++ b/solution.py
@@ -465,7 +465,7 @@
         BLOCK,
     )
     r_third = exchange(j_third)
-    v_other = [send(after([j_third], w), SIBLING) for w in v_own]
+    v_other = [send(after([far_near], w), SIBLING) for w in v_own]
 
     held = jnp.concatenate([shares_of(0)] + [x[: adp * rank] for x in told]).reshape(4 * adp, rank, SHARE)
     held = (held, send(held, SIBLING))
@@ -473,9 +473,9 @@
     name_m = jnp.where(outer, names[2], names[3])
     name_f = jnp.where(outer, names[3], names[2])
     meta = jnp.concatenate([place, names[0], names[1], name_m, name_f])
-    shrink_mine = jnp.concatenate([shrink_w, after([j_third], shrink_o)], axis=0)
+    shrink_mine = jnp.concatenate([shrink_w, after([j_partner], shrink_o)], axis=0)
     shrink_other = send(shrink_mine, SIBLING)
-    sums = shrink_sums(meta, [[hidden], [mid], [partner], [far]], [0, 2, 1, 3], shrink_mine, shrink_other, held)
+    sums = shrink_sums(meta, [[after([j_third], hidden)], [mid], [partner], [far]], [0, 2, 1, 3], shrink_mine, shrink_other, held)
     r_sums = exchange(sums)
     low, swapped = low_sums(r_sums)
     low = add(low, send(swapped, MIDDLE))

time: 355 us -> 368 us (1.037)
  starting transfers between devices: 73.8 us -> 85.9 us
    ppermute x26, waiting for transfers between devices: 160 us -> 147 us  [send(): return lax.ppermute(x, 'pool', pairs)]
    all_to_all x7, waiting for transfers between devices: 0.02 us -> 12.2 us  [exchange(): return lax.all_to_all(x, 'tensor', split_axis=0, concat_axis=0, tiled=True)]
    ppermute x26, starting transfers between devices: 44.6 us -> 56.7 us  [send(): return lax.ppermute(x, 'pool', pairs)]
  transfers between devices with their start and end apart: 33 -> 33, of which waited for: 14 -> 11; matrix products, arithmetic and copies ran while one was open for 6% -> 6% of each run, Pallas kernels for 24% -> 23%
where the time goes in v1:
time: 368 us; the launch traced here: 366 us
  waiting for transfers between devices  160 us (43%)
  Pallas kernels  90.2 us (25%)
  starting transfers between devices  85.9 us (23%)
  local copies, waits for them, and re-layouts  24.1 us (7%)
  other arithmetic  6.05 us (2%)
    ppermute x26, waiting for transfers between devices, send(): return lax.ppermute(x, 'pool', pairs)  147 us
    pallas_call x5, Pallas kernels, products(): pl.pallas_call(functools.partial(products_kernel, jobs, len(weights)), gr...  65.3 us
    ppermute x26, starting transfers between devices, send(): return lax.ppermute(x, 'pool', pairs)  56.7 us
    all_to_all x7, starting transfers between devices, exchange(): return lax.all_to_all(x, 'tensor', split_axis=0, concat_axis=0, tiled=True)  29.3 us
    pallas_call x6, Pallas kernels, finish(): pl.pallas_call(functools.partial(finish_kernel, role, row, rows, lanes, m...  13.3 us
    all_to_all x7, waiting for transfers between devices, exchange(): return lax.all_to_all(x, 'tensor', split_axis=0, concat_axis=0, tiled=True)  12.2 us
    slice x2, local copies, waits for them, and re-layouts, line_of_four(): pieces = [down_weight[lo:hi] for lo, hi in cuts]  8.02 us
  transfers between devices with their start and end apart: 33, of which 11 were waited for; matrix products, arithmetic and copies ran while one was open for 6% of the time, Pallas kernels for 23%

profile of v1, /device:TPU:0, one launch (start us, length us, event | category | flops | bytes accessed | tf_op | source)
XLA Modules:
  0.0 366.3 jit_solution(12623966913014583488)
XLA Ops:
  0.0 2.3 slice.52
  2.7 2.6 collective-permute-start.7
  5.3 2.5 collective-permute-start.8
  7.7 5.8 %fusion.7 = (bf16[1024,1024]{1,0:T(8,128)(2,1)}, bf16[1024,1024]{1,0:T(8,128)(2,1)}, bf16[1024,1024]{1,0:T(8,128)(2,1)}) fusion(bf16[3584,1024]{1,0:T(8,128)(2,1)} %refs_10_.9), kind=kLoop, calls=%fused_computation.21 | loop fusion | bytes 12582912 | tf_op jit(solution)/shard_map/slice | solution.py:429
  14.2 2.2 reshape.50
  16.5 2.0 copy.11
  18.4 4.2 %all-to-all-start = ((bf16[4,2,64,512]{3,2,1,0:T(8,128)(2,1)}), bf16[4,2,64,512]{3,2,1,0:T(8,128)(2,1)}, u32[]{:S(2)}, u32[]{:S(2)}) async-start(bf16[4,2,64,512]{3,2,1,0:T(8,128)(2,1)} %copy.11), calls=%async_computation | async-start | bytes 1048576 | tf_op jit(solution)/shard_map/all_to_all | solution.py:422
  22.7 1.3 collective-permute-done.2.refs_9_.refs_13_
  24.0 15.7 %shard_map.64 = bf16[4,128,2048]{2,1,0:T(8,128)(2,1)} custom-call(s32[3]{0:T(128)S(1)} %pad_add_fusion.meta, bf16[512,3584]{1,0:T(8,128)(2,1)} %refs_0_.2, bf16[512,3584]{1,0:T(8,128)(2,1)} %refs_0_.2, bf16[512,3584]{1,0:T(8,128)(2,1)} %refs_0_.2, bf16[512,3584]{1,0:T(8,128)(2,1)} %refs_0_.2, bf16[3584,1024]{1,0:T(8,128)(2,1)} %refs_10_.9, ...), custom_call_target="tpu_custom_call" | custom-call | flops 1000 | bytes 1000 | tf_op jit(solution)/shard_map/pallas_call | solution.py:191
  39.7 4.5 %all-to-all-start.1 = ((bf16[4,128,2048]{2,1,0:T(8,128)(2,1)}), bf16[4,128,2048]{2,1,0:T(8,128)(2,1)}, u32[]{:S(2)}, u32[]{:S(2)}) async-start(bf16[4,128,2048]{2,1,0:T(8,128)(2,1)} %shard_map.64), calls=%async_computation.1 | async-start | bytes 4194304 | tf_op jit(solution)/shard_map/all_to_all | solution.py:422
  44.2 1.8 dynamic-slice_bitcast_fusion
  46.0 2.7 collective-permute-start.4
  49.1 2.0 collective-permute-start.6
  51.1 37.5 %collective-permute-done.4 = bf16[144,512]{1,0:T(8,128)(2,1)S(1)} collective-permute-done((bf16[144,512]{1,0:T(8,128)(2,1)S(1)}, bf16[144,512]{1,0:T(8,128)(2,1)S(1)}, u32[]{:S(2)}, u32[]{:S(2)}) %collective-permute-start.4) | collective-permute-done | bytes 147488 | tf_op jit(solution)/shard_map/ppermute | solution.py:84
  88.7 10.9 %collective-permute-done.5 = bf16[144,512]{1,0:T(8,128)(2,1)S(1)} collective-permute-done((bf16[144,512]{1,0:T(8,128)(2,1)S(1)}, bf16[144,512]{1,0:T(8,128)(2,1)S(1)}, u32[]{:S(2)}, u32[]{:S(2)}) %collective-permute-start.5) | collective-permute-done | bytes 147488 | tf_op jit(solution)/shard_map/ppermute | solution.py:84
  99.6 0.7 copy-done.12
  100.2 2.5 collective-permute-start.9
  102.8 1.3 collective-permute-start.10
  104.1 9.1 %collective-permute-start.11 = (bf16[128,3584]{1,0:T(8,128)(2,1)}, bf16[128,3584]{1,0:T(8,128)(2,1)}, u32[]{:S(2)}, u32[]{:S(2)}) collective-permute-start(bf16[128,3584]{1,0:T(8,128)(2,1)} %bitcast.30), channel_id=1, source_target_pairs={{0,8},{4,12},{24,16},{28,20},{1,9},{5,13},{25,17},{29,21},{2,10},{... | collective-permute-start | bytes 2752520 | tf_op jit(solution)/shard_map/ppermute | solution.py:84
  113.2 15.7 %shard_map.65 = bf16[4,128,2048]{2,1,0:T(8,128)(2,1)} custom-call(s32[3]{0:T(128)S(1)} %pad_add_fusion.meta, bf16[512,3584]{1,0:T(8,128)(2,1)} %collective-permute-done.7.refs_0_.refs_1_.refs_2_.refs_3_, bf16[512,3584]{1,0:T(8,128)(2,1)} %collective-permute-done.7.refs_0_.refs_1_.refs_2_.refs_3_, ...), custom_call_target="tpu_custom_call" | custom-call | flops 1000 | bytes 1000 | tf_op jit(solution)/shard_map/pallas_call | solution.py:191
  128.9 4.5 %all-to-all-start.2 = ((bf16[4,128,2048]{2,1,0:T(8,128)(2,1)}), bf16[4,128,2048]{2,1,0:T(8,128)(2,1)}, u32[]{:S(2)}, u32[]{:S(2)}) async-start(bf16[4,128,2048]{2,1,0:T(8,128)(2,1)} %shard_map.65), calls=%async_computation.2 | async-start | bytes 4194304 | tf_op jit(solution)/shard_map/all_to_all | solution.py:422
  133.4 2.8 pad_maximum_fusion.refs_4_
  136.2 3.9 %collective-permute-start.20 = (bf16[1024,1024]{1,0:T(8,128)(2,1)}, bf16[1024,1024]{1,0:T(8,128)(2,1)}, u32[]{:S(2)}, u32[]{:S(2)}) collective-permute-start(bf16[1024,1024]{1,0:T(8,128)(2,1)} %get-tuple-element.47), channel_id=1, source_target_pairs={{0,8},{4,12},{24,16},{28,20},{1,9},{5,13},{25,17},{29,21},{2,10},{... | collective-permute-start | bytes 6291464 | tf_op jit(solution)/shard_map/ppermute | solution.py:84
  140.1 5.3 %shard_map.73 = bf16[4,128,2048]{2,1,0:T(8,128)(2,1)} custom-call(s32[3]{0:T(128)S(1)} %pad_add_fusion.meta, bf16[512,3584]{1,0:T(8,128)(2,1)} %collective-permute-done.8.refs_1_.refs_0_.refs_2_.refs_3_, bf16[512,3584]{1,0:T(8,128)(2,1)} %collective-permute-done.8.refs_1_.refs_0_.refs_2_.refs_3_, ...), custom_call_target="tpu_custom_call" | custom-call | flops 1000 | bytes 1000 | tf_op jit(solution)/shard_map/pallas_call | solution.py:191
  145.4 12.1 %all-to-all-done.2.refs_0_ = bf16[4,128,2048]{2,1,0:T(8,128)(2,1)} async-done(((bf16[4,128,2048]{2,1,0:T(8,128)(2,1)}), bf16[4,128,2048]{2,1,0:T(8,128)(2,1)}, u32[]{:S(2)}, u32[]{:S(2)}) %all-to-all-start.2) | async-done | bytes 2097184 | tf_op jit(solution)/shard_map/all_to_all | solution.py:422
  157.6 4.4 %all-to-all-start.5 = ((bf16[4,128,2048]{2,1,0:T(8,128)(2,1)}), bf16[4,128,2048]{2,1,0:T(8,128)(2,1)}, u32[]{:S(2)}, u32[]{:S(2)}) async-start(bf16[4,128,2048]{2,1,0:T(8,128)(2,1)} %shard_map.73), calls=%async_computation.5 | async-start | bytes 4194304 | tf_op jit(solution)/shard_map/all_to_all | solution.py:422
  162.0 0.9 slice.66
  163.0 1.7 pad_maximum_fusion.1
  164.7 0.7 fusion.6
  165.4 0.7 fusion.5
  166.2 3.2 slice.63
  169.3 18.1 %collective-permute-done.10.refs_4_.refs_5_.refs_6_.refs_7_ = bf16[512,3584]{1,0:T(8,128)(2,1)} collective-permute-done((bf16[512,3584]{1,0:T(8,128)(2,1)}, bf16[512,3584]{1,0:T(8,128)(2,1)}, u32[]{:S(2)}, u32[]{:S(2)}) %collective-permute-start.10) | collective-permute-done | bytes 3670048 | tf_op jit(solution)/shard_map/ppermute | solution.py:84
  187.4 17.0 %shard_map.66 = bf16[4,128,2048]{2,1,0:T(8,128)(2,1)} custom-call(s32[3]{0:T(128)S(1)} %pad_add_fusion.meta, bf16[512,3584]{1,0:T(8,128)(2,1)} %collective-permute-done.9.refs_0_.refs_1_.refs_2_.refs_3_, bf16[512,3584]{1,0:T(8,128)(2,1)} %collective-permute-done.9.refs_0_.refs_1_.refs_2_.refs_3_, ...), custom_call_target="tpu_custom_call" | custom-call | flops 1000 | bytes 1000 | tf_op jit(solution)/shard_map/pallas_call | solution.py:191
  204.4 4.4 %shard_map.67 = bf16[4,128,1280]{2,1,0:T(8,128)(2,1)} custom-call(s32[19]{0:T(128)S(1)} %concatenate.24.meta, bf16[512,3584]{1,0:T(8,128)(2,1)S(1)} %copy-done, bf16[512,3584]{1,0:T(8,128)(2,1)} %collective-permute-done.8.refs_1_.refs_0_.refs_2_.refs_3_, bf16[512,3584]{1,0:T(8,128)(2,1)} %collective-permute-done.7.refs_0_.refs_1_.refs_2_.refs_3_, ...), custom_call_target="tpu_custom_call" | custom-call | flops 1000 | bytes 1000 | tf_op jit(solution)/shard_map/pallas_call | solution.py:264
  208.8 3.7 %all-to-all-start.3 = ((bf16[4,128,1280]{2,1,0:T(8,128)(2,1)}), bf16[4,128,1280]{2,1,0:T(8,128)(2,1)S(1)}, u32[]{:S(2)}, u32[]{:S(2)}) async-start(bf16[4,128,1280]{2,1,0:T(8,128)(2,1)} %shard_map.67), calls=%async_computation.3 | async-start | bytes 2621440 | tf_op jit(solution)/shard_map/all_to_all | solution.py:422
  212.5 16.6 %collective-permute-start.22 = (bf16[512,1024]{1,0:T(8,128)(2,1)}, bf16[512,1024]{1,0:T(8,128)(2,1)}, u32[]{:S(2)}, u32[]{:S(2)}) collective-permute-start(bf16[512,1024]{1,0:T(8,128)(2,1)} %slice.52), channel_id=1, source_target_pairs={{0,8},{4,12},{24,16},{28,20},{1,9},{5,13},{25,17},{29,21},{2,10},{... | collective-permute-start | bytes 3145736 | tf_op jit(solution)/shard_map/ppermute | solution.py:84
  229.1 1.3 collective-permute-start.19
  230.5 1.1 copy-done.1
  231.6 4.2 %all-to-all-start.4 = ((bf16[4,128,2048]{2,1,0:T(8,128)(2,1)}), bf16[4,128,2048]{2,1,0:T(8,128)(2,1)S(1)}, u32[]{:S(2)}, u32[]{:S(2)}) async-start(bf16[4,128,2048]{2,1,0:T(8,128)(2,1)} %shard_map.66), calls=%async_computation.4 | async-start | bytes 4194304 | tf_op jit(solution)/shard_map/all_to_all | solution.py:422
  235.8 13.9 %collective-permute-done.22.refs_6_ = bf16[512,1024]{1,0:T(8,128)(2,1)} collective-permute-done((bf16[512,1024]{1,0:T(8,128)(2,1)}, bf16[512,1024]{1,0:T(8,128)(2,1)}, u32[]{:S(2)}, u32[]{:S(2)}) %collective-permute-start.22) | collective-permute-done | bytes 1048608 | tf_op jit(solution)/shard_map/ppermute | solution.py:84
  249.7 2.9 collective-permute-done.23.refs_7_
  252.6 24.7 %collective-permute-done.19.refs_2_.refs_3_ = bf16[512,2048]{1,0:T(8,128)(2,1)} collective-permute-done((bf16[512,2048]{1,0:T(8,128)(2,1)}, bf16[512,2048]{1,0:T(8,128)(2,1)}, u32[]{:S(2)}, u32[]{:S(2)}) %collective-permute-start.19) | collective-permute-done | bytes 2097184 | tf_op jit(solution)/shard_map/ppermute | solution.py:84
  277.3 11.7 %shard_map.75 = bf16[4,128,2048]{2,1,0:T(8,128)(2,1)} custom-call(s32[3]{0:T(128)S(1)} %pad_add_fusion.meta, bf16[512,3584]{1,0:T(8,128)(2,1)} %collective-permute-done.9.refs_0_.refs_1_.refs_2_.refs_3_, bf16[512,3584]{1,0:T(8,128)(2,1)} %collective-permute-done.9.refs_0_.refs_1_.refs_2_.refs_3_, bf16[512,2048]{1,0:T(8,128)(2,1)} %collective-permute-done.19.refs_2_.refs_3_, ...), custom_call_target="tpu_custom_call" | custom-call | flops 1000 | bytes 1000 | tf_op jit(solution)/shard_map/pallas_call | solution.py:191
  289.0 1.3 copy-done.4
  290.3 3.9 %all-to-all-start.6 = ((bf16[4,128,2048]{2,1,0:T(8,128)(2,1)}), bf16[4,128,2048]{2,1,0:T(8,128)(2,1)S(1)}, u32[]{:S(2)}, u32[]{:S(2)}) async-start(bf16[4,128,2048]{2,1,0:T(8,128)(2,1)} %shard_map.75), calls=%async_computation.6 | async-start | bytes 4194304 | tf_op jit(solution)/shard_map/all_to_all | solution.py:422
  294.1 1.7 shard_map.68
  297.1 1.5 shard_map.69.refs_1_
  298.7 1.3 collective-permute-start.15
  299.9 6.3 %collective-permute-done.15.refs_2_ = bf16[128,256]{1,0:T(8,128)(2,1)S(1)} collective-permute-done((bf16[128,256]{1,0:T(8,128)(2,1)}, bf16[128,256]{1,0:T(8,128)(2,1)S(1)}, u32[]{:S(2)}, u32[]{:S(2)}) %collective-permute-start.15) | collective-permute-done | bytes 65568 | tf_op jit(solution)/shard_map/ppermute | solution.py:84
  306.3 0.8 copy-done.6
  307.1 3.0 shard_map.71
  310.1 2.8 shard_map.74
  312.9 1.6 collective-permute-start.18
  314.5 2.4 shard_map.70.own
  316.9 0.8 copy-done.8
  317.7 2.1 shard_map.72
  319.8 4.3 %collective-permute-start.17 = (bf16[128,2048]{1,0:T(8,128)(2,1)}, bf16[128,2048]{1,0:T(8,128)(2,1)}, u32[]{:S(2)}, u32[]{:S(2)}) collective-permute-start(bf16[128,2048]{1,0:T(8,128)(2,1)} %shard_map.72), channel_id=1, source_target_pairs={{0,16},{4,20},{8,24},{12,28},{16,0},{20,4},{24,8},{28,12},{1,17},{... | collective-permute-start | bytes 1572872 | tf_op jit(solution)/shard_map/ppermute | solution.py:84
  324.1 1.4 shard_map.76
  325.6 1.5 collective-permute-start.24
  327.0 21.5 %collective-permute-done.17.two = bf16[128,2048]{1,0:T(8,128)(2,1)} collective-permute-done((bf16[128,2048]{1,0:T(8,128)(2,1)}, bf16[128,2048]{1,0:T(8,128)(2,1)}, u32[]{:S(2)}, u32[]{:S(2)}) %collective-permute-start.17) | collective-permute-done | bytes 524320 | tf_op jit(solution)/shard_map/ppermute | solution.py:84
  348.6 1.5 shard_map.77
  350.1 1.3 collective-permute-start.25
  352.0 10.3 %collective-permute-done.25.outer_three = bf16[128,2048]{1,0:T(8,128)(2,1)S(1)} collective-permute-done((bf16[128,2048]{1,0:T(8,128)(2,1)}, bf16[128,2048]{1,0:T(8,128)(2,1)S(1)}, u32[]{:S(2)}, u32[]{:S(2)}) %collective-permute-start.25) | collective-permute-done | bytes 524320 | tf_op jit(solution)/shard_map/ppermute | solution.py:84
  362.3 4.0 %shard_map.78 = bf16[128,8192]{1,0:T(8,128)(2,1)} custom-call(s32[19]{0:T(128)S(1)} %concatenate.24.meta, s32[1]{0:T(128)} %dynamic_slice.19.count, bf16[128,2048]{1,0:T(8,128)(2,1)S(1)} %copy-done.9, bf16[128,2048]{1,0:T(8,128)(2,1)} %collective-permute-done.16.one, bf16[128,2048]{1,0:T(8,128)(2,1)} %collective-permute-done.17.two, ...), custom_call_target="tpu_custom_call" | custom-call | flops 1000 | bytes 1000 | tf_op jit(solution)/shard_map/pallas_call | solution.py:398
  (69 shorter events, 3.9 us)
Async XLA Ops:
  2.3 11.8 %collective-permute-start.3 = (bf16[512,1024]{1,0:T(8,128)(2,1)}, bf16[512,1024]{1,0:T(8,128)(2,1)S(1)}, u32[]{:S(2)}, u32[]{:S(2)}) collective-permute-start(bf16[512,1024]{1,0:T(8,128)(2,1)} %slice.52), channel_id=1, source_target_pairs={{0,4},{4,0},{8,12},{12,8},{16,20},{20,16},{24,28},{28,24},{1,5},{5... | collective-permute-start | bytes 3145736 | tf_op jit(solution)/shard_map/ppermute | solution.py:84
  2.7 97.5 %collective-permute-start.7 = (bf16[512,3584]{1,0:T(8,128)(2,1)}, bf16[512,3584]{1,0:T(8,128)(2,1)}, u32[]{:S(2)}, u32[]{:S(2)}) collective-permute-start(bf16[512,3584]{1,0:T(8,128)(2,1)} %refs_0_.2), channel_id=1, source_target_pairs={{0,8},{4,12},{8,0},{12,4},{16,24},{20,28},{24,16},{28,20},{1,9},{5... | collective-permute-start | bytes 11010056 | tf_op jit(solution)/shard_map/ppermute | solution.py:84
  5.3 95.0 %collective-permute-start.8 = (bf16[512,3584]{1,0:T(8,128)(2,1)}, bf16[512,3584]{1,0:T(8,128)(2,1)}, u32[]{:S(2)}, u32[]{:S(2)}) collective-permute-start(bf16[512,3584]{1,0:T(8,128)(2,1)} %refs_0_.2), channel_id=1, source_target_pairs={{8,16},{12,20},{16,8},{20,12},{9,17},{13,21},{17,9},{21,13},{10,18... | collective-permute-start | bytes 11010056 | tf_op jit(solution)/shard_map/ppermute | solution.py:84
  13.5 9.2 %collective-permute-start = (bf16[1024,1024]{1,0:T(8,128)(2,1)}, bf16[1024,1024]{1,0:T(8,128)(2,1)S(1)}, u32[]{:S(2)}, u32[]{:S(2)}) collective-permute-start(bf16[1024,1024]{1,0:T(8,128)(2,1)} %get-tuple-element.55), channel_id=1, source_target_pairs={{0,4},{4,0},{8,12},{12,8},{16,20},{20,16},{24,28},{28,24},{1,5},{5... | collective-permute-start | bytes 6291464 | tf_op jit(solution)/shard_map/ppermute | solution.py:84
  13.7 9.0 %collective-permute-start.1 = (bf16[1024,1024]{1,0:T(8,128)(2,1)}, bf16[1024,1024]{1,0:T(8,128)(2,1)}, u32[]{:S(2)}, u32[]{:S(2)}) collective-permute-start(bf16[1024,1024]{1,0:T(8,128)(2,1)} %get-tuple-element.54), channel_id=1, source_target_pairs={{0,4},{4,0},{8,12},{12,8},{16,20},{20,16},{24,28},{28,24},{1,5},{5... | collective-permute-start | bytes 6291464 | tf_op jit(solution)/shard_map/ppermute | solution.py:84
  14.0 10.0 %collective-permute-start.2 = (bf16[1024,1024]{1,0:T(8,128)(2,1)}, bf16[1024,1024]{1,0:T(8,128)(2,1)}, u32[]{:S(2)}, u32[]{:S(2)}) collective-permute-start(bf16[1024,1024]{1,0:T(8,128)(2,1)} %get-tuple-element.47), channel_id=1, source_target_pairs={{0,4},{4,0},{8,12},{12,8},{16,20},{20,16},{24,28},{28,24},{1,5},{5... | collective-permute-start | bytes 6291464 | tf_op jit(solution)/shard_map/ppermute | solution.py:84
  18.4 21.2 %all-to-all-start = ((bf16[4,2,64,512]{3,2,1,0:T(8,128)(2,1)}), bf16[4,2,64,512]{3,2,1,0:T(8,128)(2,1)}, u32[]{:S(2)}, u32[]{:S(2)}) async-start(bf16[4,2,64,512]{3,2,1,0:T(8,128)(2,1)} %copy.11), calls=%async_computation | async-start | bytes 1048576 | tf_op jit(solution)/shard_map/all_to_all | solution.py:422
  22.7 164.7 %copy-start.3 = (bf16[1024,1024]{1,0:T(8,128)(2,1)}, bf16[1024,1024]{1,0:T(8,128)(2,1)S(1)}, u32[]{:S(2)}) copy-start(bf16[1024,1024]{1,0:T(8,128)(2,1)S(1)} %collective-permute-done.refs_5_.refs_9_) | copy-start | bytes 6291460
  39.7 4.5 %copy-start.14 = (s32[4]{0:T(128)S(1)}, s32[4]{0:T(128)}, u32[]{:S(2)}) copy-start(s32[4]{0:T(128)} %param.12) | copy-start | bytes 52
  39.7 89.2 %all-to-all-start.1 = ((bf16[4,128,2048]{2,1,0:T(8,128)(2,1)}), bf16[4,128,2048]{2,1,0:T(8,128)(2,1)}, u32[]{:S(2)}, u32[]{:S(2)}) async-start(bf16[4,128,2048]{2,1,0:T(8,128)(2,1)} %shard_map.64), calls=%async_computation.1 | async-start | bytes 4194304 | tf_op jit(solution)/shard_map/all_to_all | solution.py:422
  46.0 42.6 %collective-permute-start.4 = (bf16[144,512]{1,0:T(8,128)(2,1)S(1)}, bf16[144,512]{1,0:T(8,128)(2,1)S(1)}, u32[]{:S(2)}, u32[]{:S(2)}) collective-permute-start(bf16[144,512]{1,0:T(8,128)(2,1)S(1)} %get-tuple-element.63), channel_id=1, source_target_pairs={{0,8},{4,12},{8,0},{12,4},{16,24},{20,28},{24,16},{28,20},{1,9},{5... | collective-permute-start | bytes 442376 | tf_op jit(solution)/shard_map/ppermute | solution.py:84
  48.7 50.9 %collective-permute-start.5 = (bf16[144,512]{1,0:T(8,128)(2,1)S(1)}, bf16[144,512]{1,0:T(8,128)(2,1)S(1)}, u32[]{:S(2)}, u32[]{:S(2)}) collective-permute-start(bf16[144,512]{1,0:T(8,128)(2,1)S(1)} %get-tuple-element.64), channel_id=1, source_target_pairs={{0,16},{4,20},{8,24},{12,28},{16,0},{20,4},{24,8},{28,12},{1,17},{... | collective-permute-start | bytes 442376 | tf_op jit(solution)/shard_map/ppermute | solution.py:84
  49.1 50.5 %collective-permute-start.6 = (bf16[144,512]{1,0:T(8,128)(2,1)S(1)}, bf16[144,512]{1,0:T(8,128)(2,1)S(1)}, u32[]{:S(2)}, u32[]{:S(2)}) collective-permute-start(bf16[144,512]{1,0:T(8,128)(2,1)S(1)} %get-tuple-element.62), channel_id=1, source_target_pairs={{0,24},{4,28},{8,16},{12,20},{16,8},{20,12},{24,0},{28,4},{1,25},{... | collective-permute-start | bytes 442376 | tf_op jit(solution)/shard_map/ppermute | solution.py:84
  88.7 10.9 %copy-start.11 = (bf16[144,512]{1,0:T(8,128)(2,1)}, bf16[144,512]{1,0:T(8,128)(2,1)S(1)}, u32[]{:S(2)}) copy-start(bf16[144,512]{1,0:T(8,128)(2,1)S(1)} %collective-permute-done.4) | copy-start | bytes 442372
  99.6 29.3 %copy-start.10 = (bf16[144,512]{1,0:T(8,128)(2,1)}, bf16[144,512]{1,0:T(8,128)(2,1)S(1)}, u32[]{:S(2)}) copy-start(bf16[144,512]{1,0:T(8,128)(2,1)S(1)} %collective-permute-done.5) | copy-start | bytes 442372
  99.6 0.7 copy-start.12
  100.2 65.9 %collective-permute-start.9 = (bf16[512,3584]{1,0:T(8,128)(2,1)}, bf16[512,3584]{1,0:T(8,128)(2,1)}, u32[]{:S(2)}, u32[]{:S(2)}) collective-permute-start(bf16[512,3584]{1,0:T(8,128)(2,1)} %collective-permute-done.7.refs_0_.refs_1_.refs_2_.refs_3_), channel_id=1, source_target_pairs={{8,16},{12,20},{16,8},{20,12},{9,17},{13,21},{17,9},{21,13},{10,18... | collective-permute-start | bytes 11010056 | tf_op jit(solution)/shard_map/ppermute | solution.py:84
  102.8 84.6 %collective-permute-start.10 = (bf16[512,3584]{1,0:T(8,128)(2,1)}, bf16[512,3584]{1,0:T(8,128)(2,1)}, u32[]{:S(2)}, u32[]{:S(2)}) collective-permute-start(bf16[512,3584]{1,0:T(8,128)(2,1)} %collective-permute-done.8.refs_1_.refs_0_.refs_2_.refs_3_), channel_id=1, source_target_pairs={{8,0},{12,4},{16,24},{20,28},{9,1},{13,5},{17,25},{21,29},{10,2},{... | collective-permute-start | bytes 11010056 | tf_op jit(solution)/shard_map/ppermute | solution.py:84
  104.1 29.3 %collective-permute-start.11 = (bf16[128,3584]{1,0:T(8,128)(2,1)}, bf16[128,3584]{1,0:T(8,128)(2,1)}, u32[]{:S(2)}, u32[]{:S(2)}) collective-permute-start(bf16[128,3584]{1,0:T(8,128)(2,1)} %bitcast.30), channel_id=1, source_target_pairs={{0,8},{4,12},{24,16},{28,20},{1,9},{5,13},{25,17},{29,21},{2,10},{... | collective-permute-start | bytes 2752520 | tf_op jit(solution)/shard_map/ppermute | solution.py:84
  128.9 28.7 %all-to-all-start.2 = ((bf16[4,128,2048]{2,1,0:T(8,128)(2,1)}), bf16[4,128,2048]{2,1,0:T(8,128)(2,1)}, u32[]{:S(2)}, u32[]{:S(2)}) async-start(bf16[4,128,2048]{2,1,0:T(8,128)(2,1)} %shard_map.65), calls=%async_computation.2 | async-start | bytes 4194304 | tf_op jit(solution)/shard_map/all_to_all | solution.py:422
  136.2 68.2 %collective-permute-start.12 = (bf16[256,3584]{1,0:T(8,128)(2,1)}, bf16[256,3584]{1,0:T(8,128)(2,1)}, u32[]{:S(2)}, u32[]{:S(2)}) collective-permute-start(bf16[256,3584]{1,0:T(8,128)(2,1)} %pad_maximum_fusion.refs_4_), channel_id=1, source_target_pairs={{0,4},{4,0},{8,12},{12,8},{16,20},{20,16},{24,28},{28,24},{1,5},{5... | collective-permute-start | bytes 5505032 | tf_op jit(solution)/shard_map/ppermute | solution.py:84
  136.2 94.2 %collective-permute-start.20 = (bf16[1024,1024]{1,0:T(8,128)(2,1)}, bf16[1024,1024]{1,0:T(8,128)(2,1)}, u32[]{:S(2)}, u32[]{:S(2)}) collective-permute-start(bf16[1024,1024]{1,0:T(8,128)(2,1)} %get-tuple-element.47), channel_id=1, source_target_pairs={{0,8},{4,12},{24,16},{28,20},{1,9},{5,13},{25,17},{29,21},{2,10},{... | collective-permute-start | bytes 6291464 | tf_op jit(solution)/shard_map/ppermute | solution.py:84
  145.4 17.5 %slice-start = ((bf16[144,512]{1,0:T(8,128)(2,1)}), bf16[128,512]{1,0:T(8,128)(2,1)S(1)}, s32[]{:S(2)}) async-start(bf16[144,512]{1,0:T(8,128)(2,1)} %copy-done.10), calls=%async_computation.7 | async-start | bytes 262144 | tf_op jit(solution)/shard_map/slice | solution.py:470
  145.4 17.5 %slice-start.1 = ((bf16[144,512]{1,0:T(8,128)(2,1)}), bf16[128,512]{1,0:T(8,128)(2,1)S(1)}, s32[]{:S(2)}) async-start(bf16[144,512]{1,0:T(8,128)(2,1)} %copy-done.11), calls=%async_computation.8 | async-start | bytes 262144 | tf_op jit(solution)/shard_map/slice | solution.py:470
  157.6 51.2 %all-to-all-start.5 = ((bf16[4,128,2048]{2,1,0:T(8,128)(2,1)}), bf16[4,128,2048]{2,1,0:T(8,128)(2,1)}, u32[]{:S(2)}, u32[]{:S(2)}) async-start(bf16[4,128,2048]{2,1,0:T(8,128)(2,1)} %shard_map.73), calls=%async_computation.5 | async-start | bytes 4194304 | tf_op jit(solution)/shard_map/all_to_all | solution.py:422
  164.7 39.7 %collective-permute-start.13 = (bf16[8,64,512]{2,1,0:T(8,128)(2,1)}, bf16[8,64,512]{2,1,0:T(8,128)(2,1)}, u32[]{:S(2)}, u32[]{:S(2)}) collective-permute-start(bf16[8,64,512]{2,1,0:T(8,128)(2,1)} %bitcast.17.refs_6_), channel_id=1, source_target_pairs={{0,4},{4,0},{8,12},{12,8},{16,20},{20,16},{24,28},{28,24},{1,5},{5... | collective-permute-start | bytes 1572872 | tf_op jit(solution)/shard_map/ppermute | solution.py:84
  187.4 17.0 %copy-start = (bf16[512,3584]{1,0:T(8,128)(2,1)S(1)}, bf16[512,3584]{1,0:T(8,128)(2,1)}, u32[]{:S(2)}) copy-start(bf16[512,3584]{1,0:T(8,128)(2,1)} %refs_0_.2) | copy-start | bytes 11010052
  208.8 21.7 %all-to-all-start.3 = ((bf16[4,128,1280]{2,1,0:T(8,128)(2,1)}), bf16[4,128,1280]{2,1,0:T(8,128)(2,1)S(1)}, u32[]{:S(2)}, u32[]{:S(2)}) async-start(bf16[4,128,1280]{2,1,0:T(8,128)(2,1)} %shard_map.67), calls=%async_computation.3 | async-start | bytes 2621440 | tf_op jit(solution)/shard_map/all_to_all | solution.py:422
  212.5 37.1 %collective-permute-start.22 = (bf16[512,1024]{1,0:T(8,128)(2,1)}, bf16[512,1024]{1,0:T(8,128)(2,1)}, u32[]{:S(2)}, u32[]{:S(2)}) collective-permute-start(bf16[512,1024]{1,0:T(8,128)(2,1)} %slice.52), channel_id=1, source_target_pairs={{0,8},{4,12},{24,16},{28,20},{1,9},{5,13},{25,17},{29,21},{2,10},{... | collective-permute-start | bytes 3145736 | tf_op jit(solution)/shard_map/ppermute | solution.py:84
  229.1 48.1 %collective-permute-start.19 = (bf16[512,2048]{1,0:T(8,128)(2,1)}, bf16[512,2048]{1,0:T(8,128)(2,1)}, u32[]{:S(2)}, u32[]{:S(2)}) collective-permute-start(bf16[512,2048]{1,0:T(8,128)(2,1)} %slice.63), channel_id=1, source_target_pairs={{8,0},{12,4},{16,24},{20,28},{9,1},{13,5},{17,25},{21,29},{10,2},{... | collective-permute-start | bytes 6291464 | tf_op jit(solution)/shard_map/ppermute | solution.py:84
  230.4 46.8 %collective-permute-start.21 = (bf16[1024,1024]{1,0:T(8,128)(2,1)}, bf16[1024,1024]{1,0:T(8,128)(2,1)}, u32[]{:S(2)}, u32[]{:S(2)}) collective-permute-start(bf16[1024,1024]{1,0:T(8,128)(2,1)} %collective-permute-done.20.refs_4_), channel_id=1, source_target_pairs={{0,4},{4,0},{8,12},{12,8},{16,20},{20,16},{24,28},{28,24},{1,5},{5... | collective-permute-start | bytes 6291464 | tf_op jit(solution)/shard_map/ppermute | solution.py:84
  230.5 1.1 copy-start.1
  231.6 57.4 %all-to-all-start.4 = ((bf16[4,128,2048]{2,1,0:T(8,128)(2,1)}), bf16[4,128,2048]{2,1,0:T(8,128)(2,1)S(1)}, u32[]{:S(2)}, u32[]{:S(2)}) async-start(bf16[4,128,2048]{2,1,0:T(8,128)(2,1)} %shard_map.66), calls=%async_computation.4 | async-start | bytes 4194304 | tf_op jit(solution)/shard_map/all_to_all | solution.py:422
  249.7 2.9 collective-permute-start.23
  288.9 17.3 %copy-start.2 = (bf16[4,128,1280]{2,1,0:T(8,128)(2,1)S(1)}, bf16[4,128,1280]{2,1,0:T(8,128)(2,1)}, u32[]{:S(2)}) copy-start(bf16[4,128,1280]{2,1,0:T(8,128)(2,1)} %copy-done.1) | copy-start | bytes 3932164
  289.0 1.3 copy-start.4
  290.3 33.8 %all-to-all-start.6 = ((bf16[4,128,2048]{2,1,0:T(8,128)(2,1)}), bf16[4,128,2048]{2,1,0:T(8,128)(2,1)S(1)}, u32[]{:S(2)}, u32[]{:S(2)}) async-start(bf16[4,128,2048]{2,1,0:T(8,128)(2,1)} %shard_map.75), calls=%async_computation.6 | async-start | bytes 4194304 | tf_op jit(solution)/shard_map/all_to_all | solution.py:422
  295.8 0.7 collective-permute-start.14
  296.5 0.6 copy-start.13
  298.7 7.6 %collective-permute-start.15 = (bf16[128,256]{1,0:T(8,128)(2,1)}, bf16[128,256]{1,0:T(8,128)(2,1)S(1)}, u32[]{:S(2)}, u32[]{:S(2)}) collective-permute-start(bf16[128,256]{1,0:T(8,128)(2,1)} %shard_map.69.refs_1_), channel_id=1, source_target_pairs={{8,0},{12,4},{16,24},{20,28},{9,1},{13,5},{17,25},{21,29},{10,2},{... | collective-permute-start | bytes 196616 | tf_op jit(solution)/shard_map/ppermute | solution.py:84
  306.3 0.8 copy-start.6
  310.1 16.9 %collective-permute-start.16 = (bf16[128,2048]{1,0:T(8,128)(2,1)}, bf16[128,2048]{1,0:T(8,128)(2,1)}, u32[]{:S(2)}, u32[]{:S(2)}) collective-permute-start(bf16[128,2048]{1,0:T(8,128)(2,1)} %shard_map.71), channel_id=1, source_target_pairs={{0,8},{4,12},{8,0},{12,4},{16,24},{20,28},{24,16},{28,20},{1,9},{5... | collective-permute-start | bytes 1572872 | tf_op jit(solution)/shard_map/ppermute | solution.py:84
  312.9 4.8 %copy-start.5 = (bf16[4,128,2048]{2,1,0:T(8,128)(2,1)S(1)}, bf16[4,128,2048]{2,1,0:T(8,128)(2,1)}, u32[]{:S(2)}) copy-start(bf16[4,128,2048]{2,1,0:T(8,128)(2,1)} %copy-done.4) | copy-start | bytes 6291460
  312.9 14.1 %collective-permute-start.18 = (bf16[128,2048]{1,0:T(8,128)(2,1)}, bf16[128,2048]{1,0:T(8,128)(2,1)}, u32[]{:S(2)}, u32[]{:S(2)}) collective-permute-start(bf16[128,2048]{1,0:T(8,128)(2,1)} %shard_map.74), channel_id=1, source_target_pairs={{8,16},{12,20},{16,8},{20,12},{9,17},{13,21},{17,9},{21,13},{10,18... | collective-permute-start | bytes 1572872 | tf_op jit(solution)/shard_map/ppermute | solution.py:84
  316.9 0.8 copy-start.8
  317.7 6.4 %copy-start.7 = (bf16[128,256]{1,0:T(8,128)(2,1)S(1)}, bf16[128,256]{1,0:T(8,128)(2,1)}, u32[]{:S(2)}) copy-start(bf16[128,256]{1,0:T(8,128)(2,1)} %shard_map.69.refs_1_) | copy-start | bytes 196612
  319.8 28.7 %collective-permute-start.17 = (bf16[128,2048]{1,0:T(8,128)(2,1)}, bf16[128,2048]{1,0:T(8,128)(2,1)}, u32[]{:S(2)}, u32[]{:S(2)}) collective-permute-start(bf16[128,2048]{1,0:T(8,128)(2,1)} %shard_map.72), channel_id=1, source_target_pairs={{0,16},{4,20},{8,24},{12,28},{16,0},{20,4},{24,8},{28,12},{1,17},{... | collective-permute-start | bytes 1572872 | tf_op jit(solution)/shard_map/ppermute | solution.py:84
  325.5 25.9 %copy-start.15 = (s32[4]{0:T(128)S(1)}, s32[4]{0:T(128)}, u32[]{:S(2)}) copy-start(s32[4]{0:T(128)} %param.13) | copy-start | bytes 52
  325.6 36.7 %copy-start.9 = (bf16[128,2048]{1,0:T(8,128)(2,1)S(1)}, bf16[128,2048]{1,0:T(8,128)(2,1)}, u32[]{:S(2)}) copy-start(bf16[128,2048]{1,0:T(8,128)(2,1)} %copy-done.8) | copy-start | bytes 1572868
  325.6 23.0 %collective-permute-start.24 = (bf16[128,2048]{1,0:T(8,128)(2,1)S(1)}, bf16[128,2048]{1,0:T(8,128)(2,1)S(1)}, u32[]{:S(2)}, u32[]{:S(2)}) collective-permute-start(bf16[128,2048]{1,0:T(8,128)(2,1)S(1)} %shard_map.76), channel_id=1, source_target_pairs={{0,8},{4,12},{24,16},{28,20},{1,9},{5,13},{25,17},{29,21},{2,10},{... | collective-permute-start | bytes 1572872 | tf_op jit(solution)/shard_map/ppermute | solution.py:84
  350.1 12.2 %collective-permute-start.25 = (bf16[128,2048]{1,0:T(8,128)(2,1)}, bf16[128,2048]{1,0:T(8,128)(2,1)S(1)}, u32[]{:S(2)}, u32[]{:S(2)}) collective-permute-start(bf16[128,2048]{1,0:T(8,128)(2,1)} %shard_map.77), channel_id=1, source_target_pairs={{8,24},{12,28},{16,0},{20,4},{9,25},{13,29},{17,1},{21,5},{10,26},... | collective-permute-start | bytes 1572872 | tf_op jit(solution)/shard_map/ppermute | solution.py:84
